TPU v7x, 32 devices: a whole 2x2x4 slice. The times are simulated.
32 devices in a mesh: dp: 8 (over z, x), tensor: 4 (over y, core).
Axes of the slice: x: 2, y: 2, z: 4, core: 2. Of those that a mesh axis runs over, the one named last changes fastest.
Arguments:
- clips: bfloat16 [8, 16, 256, 768], P('dp', 'tensor'), may hold values from -6 to 6
- cotangent: bfloat16 [8, 16, 256, 768], P('dp', 'tensor'), may hold values from -6 to 6
- timesteps: int32 [8], P('dp'), may hold values from 0 to 999
- labels: int32 [8], P('dp'), may hold values from 0 to 100
- time_table: float32 [1000, 768], replicated, may hold values from -5 to 5
- class_table: float32 [101, 768], replicated, may hold values from -5 to 5
- attention_weights: float32 [2, 4, 768, 768], P(None, None, 'dp', 'tensor'), may hold values from -0.21650635 to 0.21650635
- attention_first: float32 [2, 4, 768, 768], P(None, None, 'dp', 'tensor'), may hold values from -32 to 32
- attention_second: float32 [2, 4, 768, 768], P(None, None, 'dp', 'tensor'), may hold values from 1.47456 to 23.59296
- ffn_weights: float32 [2, 2, 768, 3072], P(None, None, 'dp', 'tensor'), may hold values from -0.21875 to 0.21875
- ffn_first: float32 [2, 2, 768, 3072], P(None, None, 'dp', 'tensor'), may hold values from -32 to 32
- ffn_second: float32 [2, 2, 768, 3072], P(None, None, 'dp', 'tensor'), may hold values from 1.47456 to 23.59296
- modulation_weights: float32 [2, 768, 4608], P(None, ('dp', 'tensor')), may hold values from -0.21875 to 0.21875
- modulation_first: float32 [2, 768, 4608], P(None, ('dp', 'tensor')), may hold values from -32 to 32
- modulation_second: float32 [2, 768, 4608], P(None, ('dp', 'tensor')), may hold values from 1.47456 to 23.59296
- bias_vectors: float32 [2, 10752], P(None, ('dp', 'tensor')), may hold values from -1 to 1
- bias_first: float32 [2, 10752], P(None, ('dp', 'tensor')), may hold values from -32 to 32
- bias_second: float32 [2, 10752], P(None, ('dp', 'tensor')), may hold values from 1.47456 to 23.59296
Outputs:
- output: bfloat16 [8, 16, 256, 768], P('dp', 'tensor')
- input_grad: float32 [8, 16, 256, 768], P('dp', 'tensor')
- cond_grad: float32 [8, 768], P('dp')
- attention_new: float32 [2, 4, 768, 768], P(None, None, 'dp', 'tensor')
- attention_first_new: float32 [2, 4, 768, 768], P(None, None, 'dp', 'tensor')
- attention_second_new: float32 [2, 4, 768, 768], P(None, None, 'dp', 'tensor')
- attention_copy: bfloat16 [2, 4, 768, 768], P(None, None, 'dp', 'tensor')
- ffn_new: float32 [2, 2, 768, 3072], P(None, None, 'dp', 'tensor')
- ffn_first_new: float32 [2, 2, 768, 3072], P(None, None, 'dp', 'tensor')
- ffn_second_new: float32 [2, 2, 768, 3072], P(None, None, 'dp', 'tensor')
- ffn_copy: bfloat16 [2, 2, 768, 3072], P(None, None, 'dp', 'tensor')
- modulation_new: float32 [2, 768, 4608], P(None, ('dp', 'tensor'))
- modulation_first_new: float32 [2, 768, 4608], P(None, ('dp', 'tensor'))
- modulation_second_new: float32 [2, 768, 4608], P(None, ('dp', 'tensor'))
- modulation_copy: bfloat16 [2, 768, 4608], P(None, ('dp', 'tensor'))
- bias_new: float32 [2, 10752], P(None, ('dp', 'tensor'))
- bias_first_new: float32 [2, 10752], P(None, ('dp', 'tensor'))
- bias_second_new: float32 [2, 10752], P(None, ('dp', 'tensor'))
- bias_copy: bfloat16 [2, 10752], P(None, ('dp', 'tensor'))
All inputs are finite; a program needn't handle non-finite values.
Results may differ from a plain program's by a relative error of at most 0.018.
Values may be sent and summed in bfloat16 or wider, within the bound.
A program may use at most 320 MiB of HBM per device.

v0:
```python
from functools import partial

import jax
import jax.numpy as jnp
from jax import lax
from jax.experimental import pallas as pl
from jax.experimental.pallas import tpu as pltpu
from jax.sharding import PartitionSpec as P

HD = 64
PAIR = 128
PARTS = 3
STEP = 10
BETA_ONE = 0.9
BETA_TWO = 0.999
ADAM_EPS = 1e-08
MATRIX_RATE = 0.04
VECTOR_RATE = 0.2
MATRIX_DECAY = 0.1
NORM_EPS = 1e-06
GELU_A = (2.0 / 3.141592653589793) ** 0.5
GELU_B = 0.044715
BLOCKED = -1e30
VMEM_LIMIT = 60 * 1024 * 1024
BOTH = ("dp", "tensor")


def mm(left, right, dims=((1,), (0,))):
    return lax.dot_general(left, right, (dims, ((), ())), preferred_element_type=jnp.float32)


def norm_parts(value):
    average = jnp.mean(value, axis=-1, keepdims=True)
    centred = value - average
    spread = jnp.mean(centred * centred, axis=-1, keepdims=True)
    inverse = lax.rsqrt(spread + NORM_EPS)
    return centred * inverse, inverse


def norm_back(grad, shape, inverse):
    first = jnp.mean(grad, axis=-1, keepdims=True)
    second = jnp.mean(grad * shape, axis=-1, keepdims=True)
    return inverse * (grad - first - shape * second)


def rows_of(ref):
    value = ref[...]
    return value.reshape(-1, value.shape[-1])


def put(ref, value):
    ref[...] = value.reshape(ref.shape).astype(ref.dtype)


def add_rows(ref, index, value):
    ref[pl.ds(index, 1), :] += jnp.sum(value, axis=0, keepdims=True)


def half_masks(rows):
    lane = lax.broadcasted_iota(jnp.int32, (rows, PAIR), 1)
    return lane < HD


def same_patch(tokens, stride):
    row = lax.broadcasted_iota(jnp.int32, (tokens, tokens), 0)
    column = lax.broadcasted_iota(jnp.int32, (tokens, tokens), 1)
    return lax.rem(row, stride) == lax.rem(column, stride)


def swap_halves(value):
    return pltpu.roll(value, HD, 1)


def start_loads(source, target, semaphores):
    for rank in range(target.shape[0]):
        pltpu.make_async_copy(source.at[rank], target.at[rank], semaphores.at[rank]).start()


def wait_loads(target, semaphores, rank):
    pltpu.make_async_copy(target.at[rank], target.at[rank], semaphores.at[rank]).wait()


def softmax_rows(scores, axis):
    raised = jnp.exp(scores - jnp.max(scores, axis=axis, keepdims=True))
    return raised * (1.0 / jnp.sum(raised, axis=axis, keepdims=True))


def attention_forward_kernel(
    stride, hook, source, stream_ref, mod_ref, bias_ref, bias_out_ref,
    project_ref, mixed_ref, branch_ref, middle_ref, weight_ref, semaphores,
):
    ranks = weight_ref.shape[0]

    @pl.when(pl.program_id(0) == 0)
    def _():
        start_loads(source, weight_ref, semaphores)

    stream = rows_of(stream_ref).astype(jnp.float32)
    tokens, width = stream.shape
    shape, _ = norm_parts(stream)
    normed = (shape * (1.0 + mod_ref[1:2]) + mod_ref[0:1]).astype(jnp.bfloat16)
    lower = half_masks(tokens)
    allowed = same_patch(tokens, stride) if stride else None

    @pl.when(pl.program_id(0) == 0)
    def _():
        for rank in range(ranks):
            wait_loads(weight_ref, semaphores, rank)

    def mix(heads):
        scores = [mm(chosen.astype(jnp.bfloat16), key, ((1,), (1,))) for chosen, key, _ in heads]
        outs = []
        for score, (_, _, value) in zip(scores, heads):
            if stride:
                score = jnp.where(allowed, score, BLOCKED)
            outs.append(mm(softmax_rows(score, -1).astype(jnp.bfloat16), value))
        return outs

    branch = None
    for rank in range(ranks):
        hook(rank)
        project = (mm(normed, weight_ref[rank, :, : 5 * PAIR]) + bias_ref[rank]).astype(jnp.bfloat16)
        project_ref[rank] = project.reshape(project_ref.shape[1:])
        query = project[:, :PAIR].astype(jnp.float32) * HD**-0.5
        key, value = project[:, PAIR : 2 * PAIR], project[:, 2 * PAIR : 3 * PAIR]
        both = project[:, 3 * PAIR : 4 * PAIR].astype(jnp.float32)
        first, second, last = mix(
            [
                (jnp.where(lower, query, 0.0), key, value),
                (jnp.where(lower, 0.0, query), key, value),
                (
                    jnp.where(lower, both * HD**-0.5, 0.0),
                    swap_halves(both).astype(jnp.bfloat16),
                    project[:, 4 * PAIR : 5 * PAIR],
                ),
            ]
        )
        mixed = jnp.concatenate(
            [jnp.where(lower, 0.0, swap_halves(last)), jnp.where(lower, first, second)], axis=1
        ).astype(jnp.bfloat16)
        mixed_ref[rank] = mixed.reshape(mixed_ref.shape[1:])
        term = mm(mixed, weight_ref[rank, :, 4 * PAIR :], ((1,), (1,)))
        branch = term if branch is None else branch + term
    branch = branch + bias_out_ref[...]
    put(branch_ref, branch)
    put(middle_ref, stream + mod_ref[2:3] * branch)


def gelu_parts(value):
    square = value * value
    bent = jnp.tanh(value * (GELU_A + (GELU_A * GELU_B) * square))
    half = 0.5 * (1.0 + bent)
    slope = half + (0.5 * value) * (1.0 - bent * bent) * (GELU_A + (3.0 * GELU_A * GELU_B) * square)
    return value * half, slope


def turn_of(rank):
    core = lax.rem(lax.axis_index("tensor"), 2)
    return rank + (1 - core) * (1 - 2 * (rank % 2))


def ffn_forward_kernel(
    stream, turned, hook, up_source, down_source, middle_ref, mod_ref, bias_ref, bias_up_ref, hidden_ref, branch_ref, *rest
):
    if stream is None:
        result_ref, *rest = rest
    up_ref, down_ref, up_semaphores, down_semaphores = rest
    step = pl.program_id(0)
    ranks = up_ref.shape[0]

    @pl.when(step == 0)
    def _():
        start_loads(up_source, up_ref, up_semaphores)
        start_loads(down_source, down_ref, down_semaphores)

    middle = middle_ref[...]
    shape, _ = norm_parts(middle)
    second = (shape * (1.0 + mod_ref[4:5]) + mod_ref[3:4]).astype(jnp.bfloat16)

    @pl.when(step == 0)
    def _():
        for rank in range(ranks):
            wait_loads(up_ref, up_semaphores, rank)
            wait_loads(down_ref, down_semaphores, rank)

    down = None
    for rank in range(ranks):
        hook(rank)
        hidden = mm(second, up_ref[rank]) + bias_up_ref[rank]
        hidden_ref[turn_of(rank) if turned else rank] = hidden.astype(jnp.bfloat16)
        active, _ = gelu_parts(hidden)
        part = mm(active.astype(jnp.bfloat16), down_ref[rank], ((1,), (1,)))
        down = part if down is None else down + part
    down = down + bias_ref[...]
    branch_ref[...] = down.astype(jnp.bfloat16)
    result = middle + mod_ref[5:6] * down
    if stream is None:
        result_ref[...] = result.astype(result_ref.dtype)
    else:
        stream.put(step, result)


def load_rows(ref, index, chunk):
    if len(ref.shape) == 2:
        return ref[index * chunk : (index + 1) * chunk, :].astype(jnp.float32)
    blocks, _, strip, width = ref.shape
    frames = chunk // (blocks * strip)
    parts = [ref[:, index * frames + frame].reshape(blocks * strip, width) for frame in range(frames)]
    return jnp.concatenate(parts, axis=0).astype(jnp.float32)


def ffn_backward_kernel(
    split, cores, hook, up_source, down_source, grad_ref, middle_ref, branch_ref, hidden_ref, mod_ref,
    grad_middle_ref, up_sum_ref, sums_ref, *refs
):
    if cores is None:
        weight_grad_ref, *refs = refs
    (up_ref, down_ref, up_semaphores, down_semaphores,
     second_ref, low_ref, low_across_ref, active_ref, slope_ref, total_ref) = refs
    step = pl.program_id(0)
    rank = step if cores is None else cores.rank(step)
    tokens, width = middle_ref.shape
    chunk = tokens // split

    @pl.when(step == 0)
    def _():
        start_loads(up_source, up_ref, up_semaphores)
        start_loads(down_source, down_ref, down_semaphores)
        sums_ref[...] = jnp.zeros_like(sums_ref)
        up_sum_ref[...] = jnp.zeros_like(up_sum_ref)
        for index in range(split):
            rows = slice(index * chunk, (index + 1) * chunk)
            grad = load_rows(grad_ref, index, chunk)
            low = (mod_ref[5:6] * grad).astype(jnp.bfloat16)
            low_ref[rows, :] = low
            low_across_ref[:, rows] = low.T
            add_rows(sums_ref, 0, low.astype(jnp.float32))
            add_rows(sums_ref, 3, grad * branch_ref[rows, :].astype(jnp.float32))
            shape, _ = norm_parts(middle_ref[rows, :])
            second = (shape * (1.0 + mod_ref[4:5]) + mod_ref[3:4]).astype(jnp.bfloat16)
            second_ref[:, rows] = second.T

    wait_loads(up_ref, up_semaphores, rank)
    wait_loads(down_ref, down_semaphores, rank)

    for index in range(split):
        hook(index)
        rows = slice(index * chunk, (index + 1) * chunk)
        active, slope = gelu_parts(hidden_ref[0, rows, :].astype(jnp.float32))
        active_ref[rows, :] = active.astype(jnp.bfloat16)
        low = (mm(low_ref[rows, :], down_ref[rank]) * slope).astype(jnp.bfloat16)
        slope_ref[rows, :] = low
        up_sum_ref[rank] += jnp.sum(low.astype(jnp.float32), axis=0, keepdims=True)
        part = mm(low, up_ref[rank], ((1,), (1,)))
        total_ref[rows, :] = jnp.where(step == 0, 0.0, total_ref[rows, :]) + part
    hook(2)
    make_up = lambda: mm(second_ref[...], slope_ref[...])
    if cores is None:
        weight_grad_ref[0, 0] = make_up().astype(jnp.bfloat16)
    else:
        cores.put(step, 0, make_up)
        cores.send(step, 0)
    hook(3)
    make_down = lambda: mm(low_across_ref[...], active_ref[...])
    if cores is None:
        weight_grad_ref[1, 0] = make_down().astype(jnp.bfloat16)
    else:
        cores.put(step, 1, make_down)
        cores.send(step, 1)

    @pl.when(step == pl.num_programs(0) - 1)
    def _():
        for index in range(split):
            rows = slice(index * chunk, (index + 1) * chunk)
            shape, inverse = norm_parts(middle_ref[rows, :])
            grad = total_ref[rows, :]
            add_rows(sums_ref, 1, grad)
            add_rows(sums_ref, 2, grad * shape)
            back = norm_back(grad * (1.0 + mod_ref[4:5]), shape, inverse)
            grad_middle_ref[rows, :] = load_rows(grad_ref, index, chunk) + back


def attention_backward_kernel(
    stride, swap, cores, hook, source, grad_ref, stream_ref, project_ref, mixed_ref, branch_ref, mod_ref, *refs
):
    if swap is None:
        grad_stream_ref, *refs = refs
    if cores is None:
        weight_grad_ref, *refs = refs
    (sums_ref, project_sum_ref,
     weight_ref, semaphores, left_ref, right_ref, outer_ref) = refs
    step = pl.program_id(0)
    ranks = weight_ref.shape[0]

    @pl.when(step == 0)
    def _():
        start_loads(source, weight_ref, semaphores)
        sums_ref[...] = jnp.zeros_like(sums_ref)
        project_sum_ref[...] = jnp.zeros_like(project_sum_ref)

    grad_middle = rows_of(grad_ref)
    tokens, width = grad_middle.shape
    stream = rows_of(stream_ref).astype(jnp.float32)
    shape, inverse = norm_parts(stream)
    rows = pl.ds(pl.multiple_of(step * tokens, tokens), tokens)
    normed = (shape * (1.0 + mod_ref[1:2]) + mod_ref[0:1]).astype(jnp.bfloat16)
    low = (mod_ref[2:3] * grad_middle).astype(jnp.bfloat16)
    left_ref[0, :, rows] = normed.T
    left_ref[1, :, rows] = low.T
    add_rows(sums_ref, 0, low.astype(jnp.float32))
    add_rows(sums_ref, 3, grad_middle * rows_of(branch_ref).astype(jnp.float32))
    lower = half_masks(tokens)
    allowed = same_patch(tokens, stride) if stride else None
    scale = HD**-0.5

    @pl.when(step == 0)
    def _():
        for rank in range(ranks):
            wait_loads(weight_ref, semaphores, rank)

    def score_grads(heads):
        scores = [mm(key, chosen.astype(jnp.bfloat16), ((1,), (1,))) for chosen, key, _, _ in heads]
        grad_probs = [mm(value, taken.astype(jnp.bfloat16), ((1,), (1,))) for _, _, value, taken in heads]
        outs = []
        for score, grad_prob in zip(scores, grad_probs):
            if stride:
                score = jnp.where(allowed, score, BLOCKED)
            probs = softmax_rows(score, 0)
            inner = jnp.sum(grad_prob * probs, axis=0, keepdims=True)
            outs.append((probs.astype(jnp.bfloat16), (probs * (grad_prob - inner)).astype(jnp.bfloat16)))
        return outs

    grad_normed = None
    for rank in range(ranks):
        hook(rank)
        project = project_ref[rank].reshape(tokens, 5 * PAIR)
        mixed = mixed_ref[rank].reshape(tokens, 2 * PAIR)
        outer_ref[rank, rows, :] = mixed
        grad_mixed = mm(low, weight_ref[rank, :, 4 * PAIR :]).astype(jnp.bfloat16)
        query, key, value = (project[:, n * PAIR : (n + 1) * PAIR] for n in range(3))
        query_wide = query.astype(jnp.float32) * scale
        pair = grad_mixed[:, PAIR:]
        pair_wide = pair.astype(jnp.float32)
        both = project[:, 3 * PAIR : 4 * PAIR].astype(jnp.float32)
        swapped = swap_halves(both).astype(jnp.bfloat16)
        single = swap_halves(grad_mixed[:, :PAIR].astype(jnp.float32))
        heads = [
            (jnp.where(keep, query_wide, 0.0), key, value, jnp.where(keep, pair_wide, 0.0)) for keep in (lower, ~lower)
        ]
        heads.append(
            (jnp.where(lower, both * scale, 0.0), swapped, project[:, 4 * PAIR :], jnp.where(lower, single, 0.0))
        )
        solved = score_grads(heads)
        outs = [
            (mm(grad_scores, key, ((0,), (0,))), mm(grad_scores, query), mm(probs, pair))
            for probs, grad_scores in solved[:2]
        ]
        parts = [
            jnp.where(lower, one, two) * factor
            for one, two, factor in zip(outs[0], outs[1], (scale, scale, 1.0))
        ]
        probs, grad_scores = solved[2]
        parts.append(
            jnp.where(lower, mm(grad_scores, swapped, ((0,), (0,))), mm(grad_scores, swapped)) * scale
        )
        parts.append(jnp.where(lower, mm(probs, single.astype(jnp.bfloat16)), 0.0))
        whole = jnp.concatenate(parts, axis=1).astype(jnp.bfloat16)
        right_ref[rank, rows, :] = whole
        add_rows(project_sum_ref, rank, whole.astype(jnp.float32))
        term = mm(whole, weight_ref[rank, :, : 5 * PAIR], ((1,), (1,)))
        grad_normed = term if grad_normed is None else grad_normed + term
    add_rows(sums_ref, 1, grad_normed)
    add_rows(sums_ref, 2, grad_normed * shape)
    back = norm_back(grad_normed * (1.0 + mod_ref[1:2]), shape, inverse)
    if swap is None:
        put(grad_stream_ref, grad_middle + back)
    else:
        swap.put(step, grad_middle + back)

    @pl.when(step == pl.num_programs(0) - 1)
    def _():
        def weights(turn, carry):
            rank = turn if cores is None else cores.rank(turn)

            def make():
                inside = mm(left_ref[0], right_ref[rank])
                outside = mm(left_ref[1], outer_ref[rank])
                return jnp.concatenate(
                    [inside[:, : 4 * PAIR], inside[:, 4 * PAIR :] + outside[:, :PAIR], outside[:, PAIR:]], axis=1
                )

            if cores is None:
                weight_grad_ref[rank] = make().astype(jnp.bfloat16)
            else:
                cores.put(turn, 0, make)
                cores.send(turn, 0)
            return carry

        lax.fori_loop(0, ranks, weights, 0)


def fixed(shape):
    return pl.BlockSpec(shape, lambda step: (0,) * len(shape), pipeline_mode=pl.Buffered(1))


def cost(flops, moved, raised=0):
    return pl.CostEstimate(flops=int(flops), bytes_accessed=int(moved), transcendentals=int(raised))


def group_spec(shape):
    return pl.BlockSpec((shape[0], 1, shape[2], shape[3]), lambda step: (0, step, 0, 0))


def rank_spec(shape):
    return pl.BlockSpec((shape[0], shape[1], 1) + shape[3:], lambda step: (0, 0, step, 0, 0))


def attention_forward(weight, stream, mod, bias, bias_out, stride, jobs=(), collective_id=None):
    shape = stream.shape
    width = shape[-1]
    ranks = bias.shape[0]
    tokens = shape[0] * shape[1] * shape[2]
    spec = group_spec(shape)
    low = jax.ShapeDtypeStruct(shape, jnp.bfloat16)
    wide = jax.ShapeDtypeStruct(shape, jnp.float32)
    project = jax.ShapeDtypeStruct((ranks,) + shape[:3] + (5 * PAIR,), jnp.bfloat16)
    mixed = jax.ShapeDtypeStruct((ranks,) + shape[:3] + (2 * PAIR,), jnp.bfloat16)
    return call(
        partial(attention_forward_kernel, stride),
        shape[1],
        [weight, stream, mod, bias, bias_out],
        anywhere(1) + [spec, fixed(mod.shape), fixed(bias.shape), fixed(bias_out.shape)],
        [project, mixed, low, wide],
        [rank_spec(project.shape), rank_spec(mixed.shape), spec, spec],
        [pltpu.VMEM((ranks, width, 6 * PAIR), jnp.bfloat16), pltpu.SemaphoreType.DMA((ranks,))],
        jobs,
        collective_id,
        cost(8 * tokens * width * width * 1.5, tokens * width * 16),
        "attention_forward",
    )


def ffn_weights_scratch(ranks, width, part):
    return [
        pltpu.VMEM((ranks, width, part), jnp.bfloat16),
        pltpu.VMEM((ranks, width, part), jnp.bfloat16),
        pltpu.SemaphoreType.DMA((ranks,)),
        pltpu.SemaphoreType.DMA((ranks,)),
    ]


def ffn_forward(up, down, middle, mod, bias_down, bias_up, stream=None, jobs=(), collective_id=None, turned=False):
    tokens, width = middle.shape
    ranks, _, part = bias_up.shape
    steps = 4
    chunk = tokens // steps
    block = pl.BlockSpec((chunk, width), lambda step: (step, 0))
    result = [jax.ShapeDtypeStruct((tokens, width), jnp.bfloat16)] if stream is None else []
    return call(
        partial(ffn_forward_kernel, stream, turned),
        steps,
        [up, down, middle, mod, bias_down, bias_up],
        anywhere(2) + [block, fixed(mod.shape), fixed(bias_down.shape), fixed(bias_up.shape)],
        [
            jax.ShapeDtypeStruct((ranks, tokens, part), jnp.bfloat16),
            jax.ShapeDtypeStruct((tokens, width), jnp.bfloat16),
        ] + result,
        [pl.BlockSpec((ranks, chunk, part), lambda step: (0, step, 0)), block] + [block] * len(result),
        ffn_weights_scratch(ranks, width, part),
        ([] if stream is None else [stream]) + list(jobs),
        collective_id,
        cost(4.8 * tokens * width * ranks * part, tokens * width * 14, tokens * ranks * part),
        "ffn_forward",
    )


def ffn_backward(up, down, grad, middle, branch, hidden, mod, cores=None, jobs=(), collective_id=None):
    tokens, width = middle.shape
    ranks, _, part = hidden.shape
    whole = fixed((tokens, width))
    made = [jax.ShapeDtypeStruct((2, ranks, width, part), jnp.bfloat16)] if cores is None else []
    return call(
        partial(ffn_backward_kernel, 2, cores),
        ranks,
        [up, down, grad, middle, branch, hidden, mod],
        anywhere(2) + [
            fixed(grad.shape), whole, whole,
            pl.BlockSpec((1, tokens, part), lambda step: (step, 0, 0)),
            fixed(mod.shape),
        ],
        [
            jax.ShapeDtypeStruct((tokens, width), jnp.float32),
            jax.ShapeDtypeStruct((ranks, 1, part), jnp.float32),
            jax.ShapeDtypeStruct((4, width), jnp.float32),
        ] + made,
        [
            whole,
            fixed((ranks, 1, part)),
            fixed((4, width)),
        ] + [pl.BlockSpec((2, 1, width, part), lambda step: (0, step, 0, 0))] * len(made),
        ffn_weights_scratch(ranks, width, part) + [
            pltpu.VMEM((width, tokens), jnp.bfloat16),
            pltpu.VMEM((tokens, width), jnp.bfloat16),
            pltpu.VMEM((width, tokens), jnp.bfloat16),
            pltpu.VMEM((tokens, part), jnp.bfloat16),
            pltpu.VMEM((tokens, part), jnp.bfloat16),
            pltpu.VMEM((tokens, width), jnp.float32),
        ],
        ([] if cores is None else [cores]) + list(jobs),
        collective_id,
        cost(9.6 * tokens * width * ranks * part, tokens * width * 20, tokens * ranks * part),
        "ffn_backward",
    )


def attention_backward(weight, grad, stream, saved, mod, stride, swap=None, cores=None, jobs=(), collective_id=None):
    project, mixed, branch = saved
    shape = stream.shape
    width = shape[-1]
    ranks = project.shape[0]
    tokens = shape[0] * shape[1] * shape[2]
    spec = group_spec(shape)
    result = [jax.ShapeDtypeStruct(shape, jnp.float32)] if swap is None else []
    made = [jax.ShapeDtypeStruct((ranks, width, 6 * PAIR), jnp.bfloat16)] if cores is None else []
    return call(
        partial(attention_backward_kernel, stride, swap, cores),
        shape[1],
        [weight, grad, stream, project, mixed, branch, mod],
        anywhere(1) + [
            spec, spec, rank_spec(project.shape), rank_spec(mixed.shape), spec, fixed(mod.shape),
        ],
        result + made + [
            jax.ShapeDtypeStruct((4, width), jnp.float32),
            jax.ShapeDtypeStruct((ranks, 5 * PAIR), jnp.float32),
        ],
        [spec] * len(result) + [fixed((ranks, width, 6 * PAIR))] * len(made) + [
            fixed((4, width)), fixed((ranks, 5 * PAIR)),
        ],
        [
            pltpu.VMEM((ranks, width, 6 * PAIR), jnp.bfloat16),
            pltpu.SemaphoreType.DMA((ranks,)),
            pltpu.VMEM((2, width, tokens), jnp.bfloat16),
            pltpu.VMEM((ranks, tokens, 5 * PAIR), jnp.bfloat16),
            pltpu.VMEM((ranks, tokens, 2 * PAIR), jnp.bfloat16),
        ],
        [job for job in (swap, cores) if job is not None] + list(jobs),
        collective_id,
        cost(16 * tokens * width * width * 1.5, tokens * width * 20),
        "attention_backward",
    )


def pack_heads(block):
    query, key, value, outer = block
    return jnp.concatenate(
        [query[:, :PAIR], key[:, :PAIR], value[:, :PAIR], query[:, PAIR:], key[:, PAIR:],
         value[:, PAIR:], outer[:, PAIR:], outer[:, :PAIR]], axis=1
    )


def unpack_heads(packed):
    part = lambda start, size: packed[:, start : start + size]
    join = lambda first, last: jnp.concatenate([part(first, PAIR), part(last, HD)], axis=1)
    return [join(0, 3 * PAIR), join(PAIR, 3 * PAIR + HD), join(2 * PAIR, 4 * PAIR), join(5 * PAIR, 4 * PAIR + HD)]


def pack_bias(query, value, ranks):
    query, value = query.reshape(ranks, -1), value.reshape(ranks, -1)
    none = jnp.zeros((ranks, PAIR), query.dtype)
    return jnp.concatenate(
        [query[:, :PAIR], none, value[:, :PAIR], query[:, PAIR:], none[:, :HD], value[:, PAIR:], none[:, :HD]],
        axis=1,
    )[:, None]


def unpack_bias(sums):
    query = jnp.concatenate([sums[:, :PAIR], sums[:, 3 * PAIR : 3 * PAIR + HD]], axis=1)
    value = jnp.concatenate([sums[:, 2 * PAIR : 3 * PAIR], sums[:, 4 * PAIR : 4 * PAIR + HD]], axis=1)
    return query.reshape(-1), value.reshape(-1)


def place():
    return lax.axis_index("dp"), lax.axis_index("tensor"), lax.axis_size("dp"), lax.axis_size("tensor")


def greet_all():
    device, rank, dp, tp = place()
    me, count = device * tp + rank, dp * tp
    barrier = pltpu.get_barrier_semaphore()

    def greet(index, carry):
        peer = lax.rem(me + index, count)
        pl.semaphore_signal(
            barrier, inc=1, device_id=(peer // tp, lax.rem(peer, tp)), device_id_type=pl.DeviceIdType.MESH
        )
        return carry

    lax.fori_loop(1, count, greet, 0)
    pl.semaphore_wait(barrier, count - 1)


def push(source, target, send, receive, device, rank):
    pltpu.make_async_remote_copy(
        src_ref=source, dst_ref=target, send_sem=send, recv_sem=receive,
        device_id=(device, rank), device_id_type=pl.DeviceIdType.MESH,
    ).start()


def wait_bytes(ref, semaphore):
    pltpu.make_async_copy(ref, ref, semaphore).wait()


class Where:
    def __init__(self):
        device, rank = lax.axis_index("dp"), lax.axis_index("tensor")
        self.count = lax.axis_size("dp") // 2
        self.device, self.rank = device, rank
        self.far, self.side = device // 2, lax.rem(device, 2)
        self.row, self.core = rank // 2, lax.rem(rank, 2)
        self.other_side = self.far * 2 + 1 - self.side
        self.other_row = (1 - self.row) * 2 + self.core
        self.other_core = self.row * 2 + 1 - self.core

    def ahead(self, step):
        return lax.rem(self.far + step, self.count)

    def line(self, step):
        return self.ahead(step) * 2 + self.side


def greet_neighbours(here):
    barrier = pltpu.get_barrier_semaphore()
    peers = [(here.other_side, here.rank), (here.device, here.other_row), (here.device, here.other_core)]
    peers += [(here.line(step), here.rank) for step in range(1, here.count)]
    for peer in peers:
        pl.semaphore_signal(barrier, inc=1, device_id=peer, device_id_type=pl.DeviceIdType.MESH)
    pl.semaphore_wait(barrier, len(peers))


def add_into(target, left, right):
    target[...] = left[...] + right[...]


class ScatterChain:
    def __init__(self, here, kept, line, lead, scratch):
        self.here, self.kept, self.line, self.lead = here, kept, line, lead
        self.keep, self.first_one, self.last_one, self.first_two, self.last_two, self.semaphores = scratch
        self.rows = line.shape[1]

    @staticmethod
    def scratch(width, columns, dp, lead):
        rows, far = width // dp, dp // 2
        low = lambda *shape: pltpu.VMEM(shape + (columns,), jnp.bfloat16)
        return [
            low(2, width),
            low(2, lead, rows), low(2 * (far - lead) * rows), low(lead, rows), low(far - lead, rows),
            pltpu.SemaphoreType.DMA((6, 2)),
        ]

    def chunk(self, row, far, side):
        return self.keep.at[row, pl.ds(pl.multiple_of((far * 2 + side) * self.rows, self.rows), self.rows)]

    def send(self, slot, source, target, device, rank):
        push(source, target, self.semaphores.at[slot, 0], self.semaphores.at[slot, 1], device, rank)

    def arrived(self, slot, ref):
        wait_bytes(ref, self.semaphores.at[slot, 1])

    def left(self, slot, ref):
        wait_bytes(ref, self.semaphores.at[slot, 0])

    def stage_one(self):
        here, lead = self.here, self.lead
        pltpu.make_async_copy(self.kept, self.keep, self.semaphores.at[5, 0]).start()
        for row in range(2):
            for far in range(lead):
                rows = pl.ds(pl.multiple_of((far * 2 + 1 - here.side) * self.rows, self.rows), self.rows)
                self.send(1, self.kept.at[row, rows], self.first_one.at[row, far], here.other_side, here.rank)
        start, size = lead * 2 * self.rows, (here.count - lead) * 2 * self.rows
        self.send(2, self.kept.at[1 - here.row, pl.ds(start, size)], self.last_one, here.device, here.other_row)

    def stage_two(self):
        here, lead = self.here, self.lead
        wait_bytes(self.keep, self.semaphores.at[5, 0])
        self.arrived(1, self.first_one)
        for row in range(2):
            for far in range(lead):
                mine = self.chunk(row, far, here.side)
                add_into(mine, mine, self.first_one.at[row, far])
        for far in range(lead):
            self.send(3, self.chunk(1 - here.row, far, here.side), self.first_two.at[far], here.device, here.other_row)
        self.arrived(2, self.last_one)
        for far in range(lead, here.count):
            for side in range(2):
                mine = self.chunk(here.row, far, side)
                add_into(mine, mine, self.last_one.at[pl.ds(((far - lead) * 2 + side) * self.rows, self.rows)])
        for far in range(lead, here.count):
            self.send(
                4, self.chunk(here.row, far, 1 - here.side), self.last_two.at[far - lead], here.other_side, here.rank
            )

    def merge(self):
        here = self.here
        self.arrived(3, self.first_two)
        self.arrived(4, self.last_two)
        for far in range(here.count):
            land = self.first_two.at[far] if far < self.lead else self.last_two.at[far - self.lead]
            add_into(self.line.at[far], self.chunk(here.row, far, here.side), land)

    def finish(self):
        self.left(1, self.first_one)
        self.left(2, self.last_one)
        self.left(3, self.first_two)
        self.left(4, self.last_two)


class LineChain:
    def __init__(self, here, line, out, land, semaphores):
        self.here, self.line, self.out, self.land, self.semaphores = here, line, out, land, semaphores

    @staticmethod
    def scratch(far, rows, columns):
        return [pltpu.VMEM((far - 1, rows, columns), jnp.bfloat16), pltpu.SemaphoreType.DMA((2,))]

    def start(self):
        here = self.here
        for step in range(1, here.count):
            push(
                self.line.at[here.ahead(step)], self.land.at[step - 1], self.semaphores.at[0],
                self.semaphores.at[1], here.line(step), here.rank,
            )

    def finish(self):
        wait_bytes(self.land, self.semaphores.at[1])
        total = self.line[self.here.far].astype(jnp.float32)
        for step in range(1, self.here.count):
            total = total + self.land[step - 1].astype(jnp.float32)
        self.out[...] = total
        wait_bytes(self.land, self.semaphores.at[0])


def leave_kernel(mod_start, *refs):
    refs = list(refs)
    scattering = len(refs) > 10
    kept, begun, *done = [refs.pop(0) for _ in range(6 if scattering else 2)]
    if not scattering:
        refs = [kept, begun] + refs
    small_ref, modulation_ref, *refs = refs
    heads_out, wide_out = (refs.pop(0), refs.pop(0)) if scattering else (None, None)
    sum_ref, act_ref, land_ref, acting_ref, semaphores, *space = refs
    device, rank, dp, tp = place()
    me, count = device * tp + rank, dp * tp
    greet_all()
    if scattering:
        here = Where()
        line_ref, out, *space = space
        pick = lambda number: [space.pop(0) for _ in range(number)]
        chains, trails = [], []
        for index in range(PARTS):
            size = out.shape[1] // PARTS
            part = pl.ds(index * size, size)
            line = line_ref.at[index]
            chains.append(ScatterChain(here, kept.at[0, :, :, part], line, here.count // 2, pick(6)))
            trails.append(LineChain(here, line, out.at[:, part], *pick(2)))
        others = [LineChain(here, begun.at[0], wide_out.at[0, 1], *pick(2))]
        chains[0].stage_one()
    for step in range(1, tp):
        there = lax.rem(rank + step, tp)
        push(small_ref.at[there], land_ref.at[rank], semaphores.at[0], semaphores.at[1], device, there)
    land_ref[rank] = small_ref[rank]
    wait_bytes(land_ref.at[pl.ds(0, tp - 1)], semaphores.at[1])
    mine = sum_ref.at[rank]
    mine[device] = jnp.sum(land_ref[...], axis=0)

    def one(step, carry):
        push(mine.at[device], mine.at[device], semaphores.at[2], semaphores.at[3], lax.rem(device + step, dp), rank)
        return carry

    lax.fori_loop(1, dp, one, 0)
    if scattering:
        for chain in chains[1:]:
            chain.stage_one()
        for chain in others:
            chain.start()
    wait_bytes(mine.at[pl.ds(0, dp - 1)], semaphores.at[3])
    for step in range(1, tp):
        push(mine, mine, semaphores.at[4], semaphores.at[5], device, lax.rem(rank + step, tp))
    if scattering:
        for chain in chains:
            chain.stage_two()
        for chain, line in zip(chains, trails):
            chain.merge()
            line.start()
    wait_bytes(sum_ref.at[pl.ds(0, tp - 1)], semaphores.at[5])
    layers, padded, columns = modulation_ref.shape
    lines = sum_ref.shape[2]
    total = jnp.zeros((dp, padded), jnp.float32)
    for layer in range(layers):
        for index in range(columns // PAIR):
            line = layer * (tp * lines // layers) + mod_start // PAIR + index
            low = sum_ref[line // lines, :, line % lines, :].astype(jnp.bfloat16)
            total += mm(low, modulation_ref[layer, :, index * PAIR : (index + 1) * PAIR], ((1,), (1,)))
    acting_ref[...] = jnp.concatenate([total, jnp.zeros((dp, PAIR - padded), jnp.float32)], axis=1)
    act_ref[me] = acting_ref[...]

    def tell(index, carry):
        peer = lax.rem(me + index, count)
        push(acting_ref, act_ref.at[me], semaphores.at[6], semaphores.at[7], peer // tp, lax.rem(peer, tp))
        return carry

    lax.fori_loop(1, count, tell, 0)
    if scattering:
        for chain in others:
            chain.finish()
    wait_bytes(act_ref.at[pl.ds(0, count - 1)], semaphores.at[7])
    wait_bytes(act_ref.at[pl.ds(0, count - 1)], semaphores.at[6])
    wait_bytes(land_ref.at[pl.ds(0, tp - 1)], semaphores.at[0])
    wait_bytes(mine.at[pl.ds(0, dp - 1)], semaphores.at[2])
    wait_bytes(sum_ref.at[pl.ds(0, tp - 1)], semaphores.at[4])
    if scattering:
        for chain in chains + trails:
            chain.finish()
        up_first, up_last, down_last, heads_last = done
        wide_out[0, 0], wide_out[1, 0], wide_out[1, 1] = up_first[0], up_last[0], down_last[0]
        for layer, packed in enumerate((out[...], heads_last[0])):
            parts = unpack_heads(packed)
            for kind in range(4):
                heads_out[layer, kind] = parts[kind]


def leave(small, modulation, mod_start, kept, begun, done, collective_id):
    tp, lines, lanes = small.shape
    dp = lax.axis_size("dp")
    inside = pl.BlockSpec(memory_space=pltpu.VMEM)
    shapes, space, extra = [], [], []
    if kept is not None:
        _, _, width, columns = kept.shape
        rows, far, part = width // dp, dp // 2, columns // PARTS
        extra = [kept, begun, *done]
        shapes = [
            jax.ShapeDtypeStruct((2, 4, rows, columns // 4), jnp.float32),
            jax.ShapeDtypeStruct((2, 2, rows, columns), jnp.float32),
        ]
        space = [pltpu.VMEM((PARTS, far, rows, part), jnp.bfloat16), pltpu.VMEM((rows, columns), jnp.float32)]
        for _ in range(PARTS):
            space += ScatterChain.scratch(width, part, dp, far // 2) + LineChain.scratch(far, rows, part)
        space += LineChain.scratch(far, rows, columns)
    return pl.pallas_call(
        partial(leave_kernel, mod_start),
        in_specs=([pl.BlockSpec(memory_space=pl.ANY)] + [inside] * 5)[: len(extra)] + [inside, inside],
        out_specs=[inside] * (len(shapes) + 2),
        out_shape=shapes + [
            jax.ShapeDtypeStruct((tp, dp, lines, lanes), jnp.float32),
            jax.ShapeDtypeStruct((dp * tp, dp, lanes), jnp.float32),
        ],
        scratch_shapes=[
            pltpu.VMEM((tp, lines, lanes), jnp.float32),
            pltpu.VMEM((dp, lanes), jnp.float32),
            pltpu.SemaphoreType.DMA((8,)),
        ] + space,
        compiler_params=pltpu.CompilerParams(
            collective_id=collective_id, has_side_effects=True, vmem_limit_bytes=VMEM_LIMIT
        ),
        name="leave",
    )(*extra, small, modulation)


class GatherChain:
    def __init__(self, here, source, out, semaphores, half=None):
        self.here, self.source, self.out, self.semaphores = here, source, out, semaphores
        self.half = here.count // 2 if half is None else half

    @staticmethod
    def scratch():
        return [pltpu.SemaphoreType.DMA((9, 2))]

    def pieces(self, rank, side, first=0, last=None):
        last = self.here.count if last is None else last
        return self.out.at[rank, pl.ds(first, last - first), side]

    def send(self, slot, pieces, device, rank):
        push(pieces, pieces, self.semaphores.at[slot, 0], self.semaphores.at[slot, 1], device, rank)

    def wait(self, slot, way, pieces):
        wait_bytes(self.pieces(0, 0, 0, pieces), self.semaphores.at[slot, way])

    def stage_line(self):
        here = self.here
        mine = self.out.at[here.rank, here.far, here.side]
        pltpu.make_async_copy(self.source, mine, self.semaphores.at[8, 0]).start()
        for step in range(1, here.count):
            push(
                self.source, mine, self.semaphores.at[0, 0], self.semaphores.at[0, 1], here.line(step), here.rank
            )

    def line_arrived(self):
        self.wait(8, 0, 1)
        self.wait(0, 1, self.here.count - 1)

    def line_left(self):
        self.wait(0, 0, self.here.count - 1)

    def stage_near(self):
        here = self.here
        mine = self.pieces(here.rank, here.side)
        self.send(1, mine, here.other_side, here.rank)
        self.send(2, mine, here.device, here.other_row)
        self.send(3, mine, here.device, here.other_core)

    def stage_across(self):
        here, count = self.here, self.here.count
        self.wait(1, 1, count)
        self.send(4, self.pieces(here.rank, 1 - here.side, 0, self.half), here.device, here.other_row)
        self.wait(2, 1, count)
        self.send(5, self.pieces(here.other_row, here.side, self.half, count), here.other_side, here.rank)
        self.send(6, self.pieces(here.rank, 1 - here.side), here.device, here.other_core)
        self.send(7, self.pieces(here.other_row, here.side), here.device, here.other_core)

    def stage_core(self):
        here, count = self.here, self.here.count
        self.wait(4, 1, self.half)
        self.wait(5, 1, count - self.half)
        self.send(8, self.pieces(here.other_row, 1 - here.side), here.device, here.other_core)

    def finish(self):
        count, half = self.here.count, self.half
        for slot in (3, 6, 7, 8):
            self.wait(slot, 1, count)
        for slot, pieces in ((1, count), (2, count), (3, count), (4, half), (5, count - half), (6, count), (7, count)):
            self.wait(slot, 0, pieces)
        self.wait(8, 0, count)


def column_parts(here, source, out, semaphores, half=None):
    size = out.shape[4] // PARTS
    chains = []
    for index, semaphore in enumerate(semaphores):
        part = pl.ds(index * size, size)
        shard = None if source is None else source.at[:, part]
        chains.append(GatherChain(here, shard, out.at[:, :, :, :, part], semaphore, half))
    return chains


class Job:
    operands, sources, shapes, specs, aliases, space = (), None, (), (), {}, ()
    stages, last = {}, ()


def anywhere(count):
    return [pl.BlockSpec(memory_space=pl.ANY)] * count


class CoreJob(Job):
    def __init__(self, kinds, width, columns):
        block = (kinds, width, columns)
        self.shapes, self.specs = [jax.ShapeDtypeStruct((kinds, 2, width, columns), jnp.bfloat16)], anywhere(1)
        self.space = [
            pltpu.VMEM((2,) + block, jnp.bfloat16),
            pltpu.VMEM((2,) + block, jnp.bfloat16),
            pltpu.SemaphoreType.DMA((4, kinds)),
        ]

    def bind(self, here, inputs, outputs, space):
        self.here, self.kept, (self.buffer, self.land, self.semaphores) = here, outputs[0], space
        self.stages = {}
        self.last = [
            partial(self.sent, own, kind) for own in range(2) for kind in range(self.buffer.shape[1])
        ]

    def sent(self, own, kind):
        wait_bytes(self.buffer.at[own, kind], self.semaphores.at[own, kind])

    def rank(self, turn):
        return turn_of(turn)

    def put(self, turn, kind, make):
        row, own = turn // 2, lax.rem(turn, 2)

        @pl.when(turn >= 2)
        def _():
            self.sent(own, kind)

        @pl.when(own == 0)
        def _():
            self.buffer[0, kind] = make().astype(jnp.bfloat16)

        @pl.when(own == 1)
        def _():
            wait_bytes(self.land.at[row, kind], self.semaphores.at[2 + row, kind])
            self.buffer[1, kind] = (make() + self.land[row, kind].astype(jnp.float32)).astype(jnp.bfloat16)

    def send(self, turn, kind):
        here, row, own = self.here, turn // 2, lax.rem(turn, 2)

        @pl.when(own == 0)
        def _():
            push(
                self.buffer.at[0, kind], self.land.at[row, kind], self.semaphores.at[0, kind],
                self.semaphores.at[2 + row, kind], here.device, here.other_core,
            )

        @pl.when(own == 1)
        def _():
            pltpu.make_async_copy(
                self.buffer.at[1, kind], self.kept.at[kind, row], self.semaphores.at[1, kind]
            ).start()


class ScatterJob(Job):
    def __init__(self, grads, lead, close=False):
        _, _, width, columns = grads[0][0].shape
        dp = lax.axis_size("dp")
        far, rows = dp // 2, width // dp
        self.lead, self.close, self.kinds = lead, close, [kind for _, kind in grads]
        self.operands = [array for array, _ in grads]
        shape = (len(grads) - close, far, rows, columns)
        self.shapes, self.specs = [jax.ShapeDtypeStruct(shape, jnp.bfloat16)], [fixed(shape)]
        self.space = ScatterChain.scratch(width, columns, dp, lead) * len(grads)
        if close:
            self.shapes.append(jax.ShapeDtypeStruct((1, rows, columns), jnp.float32))
            self.specs.append(fixed((1, rows, columns)))
            self.space = [pltpu.VMEM((far, rows, columns), jnp.bfloat16)] + LineChain.scratch(
                far, rows, columns
            ) + self.space

    def bind(self, here, inputs, outputs, space):
        lines = [outputs[0].at[index] for index in range(outputs[0].shape[0])]
        if self.close:
            own, land, semaphores, *space = space
            lines.insert(0, own)
            line = LineChain(here, own, outputs[1].at[0], land, semaphores)
        size = len(space) // len(inputs)
        chains = [
            ScatterChain(
                here, inputs[index].at[kind], lines[index], self.lead, space[index * size : (index + 1) * size]
            )
            for index, kind in enumerate(self.kinds)
        ]
        one = chains[0]
        if len(chains) == 1:
            self.stages = {(0, 0): [one.stage_one], (2, 0): [one.stage_two]}
            self.last = [one.merge, one.finish]
            return
        two = chains[1]
        if self.close:
            self.stages = {
                (0, 0): [one.stage_one], (1, 2): [one.stage_two], (2, 0): [one.merge, line.start, two.stage_one],
                (3, 2): [two.stage_two],
            }
            self.last = [line.finish, two.merge, one.finish, two.finish]
            return
        self.stages = {
            (0, 0): [one.stage_one, two.stage_one], (1, 3): [one.stage_two], (3, 1): [two.stage_two],
        }
        self.last = [one.merge, two.merge, one.finish, two.finish]


class LineJob(Job):
    def __init__(self, line):
        kinds, far, rows, columns = line.shape
        shape = (kinds, rows, columns)
        self.operands, self.sources = [line], [fixed(line.shape)]
        self.shapes, self.specs = [jax.ShapeDtypeStruct(shape, jnp.float32)], [fixed(shape)]
        self.space = LineChain.scratch(far, rows, columns) * kinds

    def bind(self, here, inputs, outputs, space):
        chains = [
            LineChain(here, inputs[0].at[kind], outputs[0].at[kind], *space[2 * kind : 2 * kind + 2])
            for kind in range(outputs[0].shape[0])
        ]
        self.stages = {(0, 0): [chain.start for chain in chains]}
        self.last = [chain.finish for chain in chains]


class FlowJob(Job):
    def __init__(self, spread, lines, half=None, late=()):
        dp, tp = lax.axis_size("dp"), lax.axis_size("tensor")
        self.counts, self.half = (len(spread), len(late)), half
        shards = list(late) + list(lines)
        self.operands = list(spread) + shards
        self.shapes = [jax.ShapeDtypeStruct(v.shape, v.dtype) for v in spread]
        self.shapes += [jax.ShapeDtypeStruct((tp, dp // 2, 2) + v.shape, v.dtype) for v in shards]
        self.specs = anywhere(len(self.shapes))
        self.aliases = {index: index for index in range(len(spread))}
        self.space = GatherChain.scratch() * (PARTS * len(self.shapes))

    def bind(self, here, inputs, outputs, space):
        first, late = self.counts
        chains = [
            column_parts(
                here, inputs[index] if index >= first else None, outputs[index],
                space[index * PARTS : (index + 1) * PARTS], self.half,
            )
            for index in range(len(inputs))
        ]
        spread, late, lines = (
            [chain for group in chosen for chain in group]
            for chosen in (chains[:first], chains[first : first + late], chains[first + late :])
        )
        self.stages = {(0, 0): [chain.stage_near for chain in spread]}
        self.stages[0, 0] += [chain.stage_line for chain in late + lines]
        for index, spot in zip(range(PARTS), ((1, 1), (2, 0), (3, 0))):
            self.stages[spot] = [chain.stage_across for chain in spread[index::PARTS]]
            for chain in late[index::PARTS]:
                self.stages[spot] += [chain.line_arrived, chain.stage_near]
        self.last = [chain.stage_across for chain in late]
        self.last += [chain.stage_core for chain in spread + late]
        self.last += [chain.finish for chain in spread + late]
        self.last += [chain.line_arrived for chain in lines]
        self.last += [chain.line_left for chain in late + lines]


class SwapJob(Job):
    def __init__(self, tokens, to_frames):
        self.to_frames = to_frames
        self.operands = [tokens]
        shape = tokens.shape
        shape = (shape[2], shape[0], shape[1]) + shape[3:] if to_frames else (shape[1], shape[2], shape[0]) + shape[3:]
        self.shapes, self.specs = [jax.ShapeDtypeStruct(shape, tokens.dtype)], anywhere(1)
        self.space = [pltpu.SemaphoreType.DMA((3,))]

    def bind(self, here, inputs, outputs, space):
        source, out, semaphores = inputs[0], outputs[0], space[0]
        frames, ranks = out.shape[:2] if self.to_frames else (out.shape[2], out.shape[0])
        few = pl.ds(0, ranks - 1)
        most, mine = (out.at[:, few], out.at[:, 0]) if self.to_frames else (out.at[few], out.at[0])

        def ends(frame, there):
            if self.to_frames:
                return source.at[there, :, frame], out.at[frame, here.rank]
            return source.at[frame, there], out.at[here.rank, :, frame]

        def start():
            for frame in range(frames):
                pltpu.make_async_copy(*ends(frame, here.rank), semaphores.at[2]).start()
            for step in range(1, ranks):
                there = lax.rem(here.rank + step, ranks)
                for frame in range(frames):
                    push(*ends(frame, there), semaphores.at[0], semaphores.at[1], here.device, there)

        def finish():
            wait_bytes(mine, semaphores.at[2])
            wait_bytes(most, semaphores.at[1])
            wait_bytes(most, semaphores.at[0])

        self.stages, self.last = {(0, 0): [start]}, [finish]


class StreamJob(Job):
    def __init__(self, shape, frames):
        self.shape, self.frames = shape, frames
        self.shapes, self.specs = [jax.ShapeDtypeStruct(shape, jnp.bfloat16)], anywhere(1)
        ranks, groups, rows, width = shape
        block = (groups, ranks, rows, width)
        if frames:
            block = (frames, ranks, groups, rows // frames, width)
        self.space = [pltpu.VMEM(block, jnp.bfloat16), pltpu.SemaphoreType.DMA((3,))]

    def bind(self, here, inputs, outputs, space):
        self.here, self.out = here, outputs[0]
        self.buffer, self.semaphores = space
        ranks = self.shape[0]

        def finish():
            wait_bytes(self.out.at[0], self.semaphores.at[2])
            wait_bytes(self.out.at[pl.ds(0, ranks - 1)], self.semaphores.at[1])
            wait_bytes(self.out.at[pl.ds(0, ranks - 1)], self.semaphores.at[0])

        self.stages, self.last = {}, [finish]

    def put(self, step, value):
        here, ranks = self.here, self.shape[0]
        size = self.buffer.size // self.buffer.shape[0] // value.shape[1]
        if value.shape[0] > size:
            count = value.shape[0] // size
            for index in range(count):
                self.put(step * count + index, value[index * size : (index + 1) * size])
            return
        self.buffer[step] = value.reshape(self.buffer.shape[1:]).astype(jnp.bfloat16)
        if self.frames:
            strip = self.buffer.shape[3]
            target = self.out.at[here.rank, :, pl.ds(pl.multiple_of(step * strip, strip), strip)]
        else:
            target = self.out.at[here.rank, step]
        pltpu.make_async_copy(self.buffer.at[step, here.rank], target, self.semaphores.at[2]).start()
        for ahead in range(1, ranks):
            there = lax.rem(here.rank + ahead, ranks)
            push(
                self.buffer.at[step, there], target, self.semaphores.at[0], self.semaphores.at[1],
                here.device, there,
            )


def greet_jobs(here):
    barrier = pltpu.get_barrier_semaphore()
    ranks = lax.axis_size("tensor")
    peers = [(here.other_side, here.rank)]
    peers += [(here.line(step), here.rank) for step in range(1, here.count)]
    peers += [(here.device, lax.rem(here.rank + step, ranks)) for step in range(1, ranks)]
    for peer in peers:
        pl.semaphore_signal(barrier, inc=1, device_id=peer, device_id_type=pl.DeviceIdType.MESH)
    pl.semaphore_wait(barrier, len(peers))


def call(body, steps, arguments, in_specs, out_shape, out_specs, scratch, jobs, collective_id, estimate, name):
    operands = [v for job in jobs for v in job.operands]
    sources = [v for job in jobs for v in (job.sources or anywhere(len(job.operands)))]
    shapes = [v for job in jobs for v in job.shapes]
    specs = [v for job in jobs for v in job.specs]
    space = [v for job in jobs for v in job.space]
    aliases, before, after = {}, len(arguments), len(out_shape)
    for job in jobs:
        for source, target in job.aliases.items():
            aliases[before + source] = after + target
        before, after = before + len(job.operands), after + len(job.shapes)

    def kernel(*refs):
        refs = list(refs)
        take = lambda number: [refs.pop(0) for _ in range(number)]
        inputs, job_inputs = take(len(arguments)), take(len(operands))
        outputs, job_outputs = take(len(out_shape)), take(len(shapes))
        own, job_space = take(len(scratch)), refs
        step = pl.program_id(0)
        if jobs:
            here = Where()
            for job in jobs:
                pick = lambda pool, number: [pool.pop(0) for _ in range(number)]
                job.bind(
                    here, pick(job_inputs, len(job.operands)), pick(job_outputs, len(job.shapes)),
                    pick(job_space, len(job.space)),
                )

        def hook(spot):
            for index in range(steps):
                todo = [
                    stage
                    for job in jobs
                    for (late, place), stages in sorted(job.stages.items())
                    if (late * 4 + place) * steps // 4 == index * 4 + spot
                    for stage in stages
                ]
                if todo or (jobs and spot == 0 and index == 0):

                    @pl.when(step == index)
                    def _():
                        if index == 0 and spot == 0:
                            greet_jobs(here)
                        for stage in todo:
                            stage()

        hook(0)
        body(lambda spot: hook(spot) if spot else None, *inputs, *outputs, *own)
        if jobs:

            @pl.when(step == steps - 1)
            def _():
                for job in jobs:
                    for stage in job.last:
                        stage()

    more = {"collective_id": collective_id, "has_side_effects": True} if jobs else {}
    return pl.pallas_call(
        kernel,
        grid=(steps,),
        in_specs=list(in_specs) + sources,
        out_specs=list(out_specs) + specs,
        out_shape=list(out_shape) + shapes,
        scratch_shapes=list(scratch) + space,
        input_output_aliases=aliases,
        compiler_params=pltpu.CompilerParams(
            vmem_limit_bytes=VMEM_LIMIT, dimension_semantics=("arbitrary",), **more
        ),
        cost_estimate=estimate,
        name=name,
    )(*arguments, *operands)


def entry_kernel(
    per_device, row_ref, modulation_ref, *refs
):
    gather = 2 if len(refs) > 5 else 0
    refs = list(refs)
    sources = [refs.pop(0) for _ in range(gather)]
    gathered_ref, mod_ref = refs.pop(0), refs.pop(0)
    targets = [refs.pop(0) for _ in range(gather)]
    part_ref, land_ref, semaphores, *space = refs
    device, rank, dp, tp = place()
    me, count = device * tp + rank, dp * tp
    lines = land_ref.shape[1]
    if gather:
        here = Where()
        parts = column_parts(here, sources[0], targets[0], space[:PARTS])
        following = GatherChain(here, sources[1], targets[1], space[PARTS])
    greet_all()

    def tell(index, carry):
        peer = lax.rem(me + index, count)
        push(
            row_ref, gathered_ref.at[me], semaphores.at[0], semaphores.at[1], peer // tp, lax.rem(peer, tp)
        )
        return carry

    lax.fori_loop(1, count, tell, 0)
    gathered_ref[me] = row_ref[...]
    if gather:
        for chain in parts:
            chain.stage_line()
    wait_bytes(gathered_ref.at[pl.ds(0, count - 1)], semaphores.at[1])
    padded = modulation_ref.shape[1]
    width = dp * tp * per_device
    chosen = jnp.zeros((count, padded), jnp.float32)
    row = lax.broadcasted_iota(jnp.int32, (PAIR, padded), 0)
    column = lax.broadcasted_iota(jnp.int32, (PAIR, padded), 1)
    for index in range(width // PAIR):
        match = (row + index * PAIR == column + me * per_device) & (column < per_device)
        chosen += mm(
            gathered_ref[:, index, :].astype(jnp.bfloat16), jnp.where(match, 1.0, 0.0).astype(jnp.bfloat16)
        )
    clip = lax.broadcasted_iota(jnp.int32, (dp, count), 0)
    member = lax.broadcasted_iota(jnp.int32, (dp, count), 1)
    leaders = jnp.where(member == clip * tp, 1.0, 0.0).astype(jnp.bfloat16)
    rows = mm(leaders, chosen.astype(jnp.bfloat16)).astype(jnp.bfloat16)
    for layer in range(modulation_ref.shape[0]):
        part = mm(rows, modulation_ref[layer])
        size = part.shape[1] // PAIR
        for index in range(size):
            line = layer * size + index
            part_ref[:, line // lines, line % lines, :] = part[:, index * PAIR : (index + 1) * PAIR]

    def share(index, carry):
        peer = lax.rem(me + index, count)
        there, lane = peer // tp, lax.rem(peer, tp)
        push(part_ref.at[there, lane], land_ref.at[me], semaphores.at[2], semaphores.at[3], there, lane)
        return carry

    lax.fori_loop(1, count, share, 0)
    land_ref[me] = part_ref[device, rank]
    if gather:
        for chain in parts:
            chain.line_arrived()
            chain.stage_near()
        following.stage_line()
        for chain in parts:
            chain.stage_across()
    wait_bytes(land_ref.at[pl.ds(0, count - 1)], semaphores.at[3])
    mod_ref[rank] = jnp.sum(land_ref[...], axis=0)
    for step in range(1, tp):
        push(
            mod_ref.at[rank], mod_ref.at[rank], semaphores.at[4], semaphores.at[5], device, lax.rem(rank + step, tp)
        )
    if gather:
        for chain in parts:
            chain.stage_core()
    wait_bytes(gathered_ref.at[pl.ds(0, count - 1)], semaphores.at[0])
    wait_bytes(land_ref.at[pl.ds(0, count - 1)], semaphores.at[2])
    wait_bytes(mod_ref.at[pl.ds(0, tp - 1)], semaphores.at[5])
    wait_bytes(mod_ref.at[pl.ds(0, tp - 1)], semaphores.at[4])
    if gather:
        following.line_arrived()
        for chain in parts:
            chain.finish()
        for chain in (*parts, following):
            chain.line_left()


def enter(row, modulation, per_device, weights, collective_id):
    dp, tp = lax.axis_size("dp"), lax.axis_size("tensor")
    count = dp * tp
    lines = modulation.shape[0] * modulation.shape[2] // (tp * PAIR)
    inside = pl.BlockSpec(memory_space=pltpu.VMEM)
    job = FlowJob((), weights) if weights else Job()
    return pl.pallas_call(
        partial(entry_kernel, per_device),
        in_specs=[inside, inside] + anywhere(len(job.operands)),
        out_specs=[inside, inside] + list(job.specs),
        out_shape=[
            jax.ShapeDtypeStruct((count,) + row.shape, jnp.float32),
            jax.ShapeDtypeStruct((tp, lines, PAIR), jnp.float32),
        ] + list(job.shapes),
        scratch_shapes=[
            pltpu.VMEM((dp, tp, lines, PAIR), jnp.float32),
            pltpu.VMEM((count, lines, PAIR), jnp.float32),
            pltpu.SemaphoreType.DMA((6,)),
        ] + (GatherChain.scratch() * (PARTS + 1) if weights else []),
        compiler_params=pltpu.CompilerParams(
            collective_id=collective_id, has_side_effects=True, vmem_limit_bytes=VMEM_LIMIT
        ),
        name="enter",
    )(row, modulation, *job.operands)


def adam_update(weight, first, second, grad, rate, decay):
    first_new = BETA_ONE * first + (1.0 - BETA_ONE) * grad
    second_new = BETA_TWO * second + (1.0 - BETA_TWO) * grad * grad
    corrected = (
        first_new
        / (1.0 - BETA_ONE**STEP)
        / (jnp.sqrt(second_new / (1.0 - BETA_TWO**STEP)) + ADAM_EPS)
    )
    weight_new = weight - rate * (corrected + decay * weight)
    return (weight_new, first_new, second_new, weight_new.astype(jnp.bfloat16))


def dot32(form, left, right):
    return jnp.einsum(form, left, right, preferred_element_type=jnp.float32)


def exchange(blocks):
    return lax.all_to_all(blocks, "tensor", split_axis=0, concat_axis=0, tiled=True)


def gather_plain(shard):
    rows, width = shard.shape
    whole = lax.all_gather(shard, ("tensor", "dp"), axis=0, tiled=True)
    return whole.reshape(-1, lax.axis_size("dp") * rows, width)


def scatter_plain(grads):
    kinds, ranks, width, cols = grads.shape
    flat = grads.reshape(kinds, ranks * width, cols)
    summed = lax.psum_scatter(flat, ("tensor", "dp"), scatter_dimension=1, tiled=True)
    return summed.astype(jnp.float32)


def per_device(
    clips, cotangent, timesteps, labels, time_table, class_table,
    attention_weights, attention_first, attention_second,
    ffn_weights, ffn_first, ffn_second,
    modulation_weights, modulation_first, modulation_second,
    bias_vectors, bias_first, bias_second,
):
    layers, kinds, rows, cols = attention_weights.shape
    _, frames, patches, width = clips.shape
    mod_rows = modulation_weights.shape[1]
    bias_cols = bias_vectors.shape[1]
    dp, tp = lax.axis_size("dp"), lax.axis_size("tensor")
    position = lax.axis_index("dp") * tp + lax.axis_index("tensor")
    tokens = frames * patches
    strip = patches // (tp * frames)
    blocks = (tp, frames, frames * strip, width)
    pieces = (tp * frames, frames, strip, width)

    embed = time_table[timesteps] + class_table[labels]
    cond_act = jax.nn.silu(embed).astype(jnp.bfloat16)
    fused = rows % 16 == 0
    shards = [
        (
            pack_heads(attention_weights[layer].astype(jnp.bfloat16)),
            ffn_weights[layer, 0].astype(jnp.bfloat16),
            ffn_weights[layer, 1].astype(jnp.bfloat16),
        )
        for layer in range(layers)
    ]
    low = bias_vectors.astype(jnp.bfloat16).reshape(-1)
    row = jnp.concatenate([cond_act[0], low]).astype(jnp.float32)
    row = jnp.pad(row, (0, -row.shape[0] % 1024)).reshape(-1, 128)
    modulation_low = modulation_weights.astype(jnp.bfloat16)
    modulation_low = jnp.pad(modulation_low, ((0, 0), (0, -mod_rows % 32), (0, 0)))
    gathered, mod, *begun = enter(row, modulation_low, mod_rows, shards[0][:2] if fused else None, 0)
    gathered = gathered.reshape(dp * tp, -1)
    cond_all = gathered[::tp, :width].astype(jnp.bfloat16)
    bias_low = gathered[:, width : width + layers * bias_cols].reshape(dp * tp, layers, bias_cols)
    bias_low = bias_low.transpose(1, 0, 2).reshape(layers, -1)
    cond_rows = lax.dynamic_slice_in_dim(cond_all, position * mod_rows, mod_rows, axis=1)
    cond_rows = jnp.pad(cond_rows, ((0, 0), (0, -mod_rows % 32)))
    mod = mod.reshape(layers, -1)
    mod_width = mod.shape[-1]
    mod = (mod + bias_low[:, -mod_width:]).reshape(layers, 6, width)
    hidden_width = bias_low.shape[1] - mod_width - 4 * width
    bias_up = bias_low[:, 3 * width : 3 * width + hidden_width].reshape(layers, tp, 1, -1)
    bias_out = bias_low[:, None, 2 * width : 3 * width]
    bias_down = bias_low[:, None, 3 * width + hidden_width : 4 * width + hidden_width]
    bias_project = [
        pack_bias(bias_low[layer, :width], bias_low[layer, width : 2 * width], tp) for layer in range(layers)
    ]

    by_patch = lambda v: v.reshape(frames, tp * frames, strip, width).transpose(1, 0, 2, 3)
    first = clips[0].reshape(1, frames, patches, width)

    whole = lambda weight: weight.reshape(tp, width, -1)
    attend = lambda layer, weight, stream, stride, *more: attention_forward(
        whole(weight), stream, mod[layer], bias_project[layer], bias_out[layer], stride, *more
    )
    expand = lambda layer, up, down, middle, *more: ffn_forward(
        whole(up), whole(down), middle.reshape(tokens, width), mod[layer], bias_down[layer], bias_up[layer], *more
    )
    if fused:
        attention_a, up_a = begun
        *heads_a, middle_a, up_a, down_a, attention_b = attend(
            0, attention_a, first, 0, [FlowJob([up_a], [shards[1][0]], None, [shards[0][2]])], 1
        )
        hidden_a, pushed_a, second, attention_b, up_b, down_b = expand(
            0, up_a, down_a, middle_a, StreamJob(blocks, frames),
            [FlowJob([attention_b], [shards[1][2]], dp // 8, [shards[1][1]])], 2, True,
        )
        *heads_b, middle_b, down_b = attend(1, attention_b, second, strip, [FlowJob([down_b], [])], 3)
        cot = cotangent.reshape(frames, tp, frames, strip, width)
        hidden_b, pushed_b, result, cot = expand(
            1, up_b, down_b, middle_b, None, [SwapJob(cot, False)], 4, True
        )
        attention_a, up_a, down_a = whole(attention_a), whole(up_a), whole(down_a)
        attention_b, up_b, down_b = whole(attention_b), whole(up_b), whole(down_b)
    else:
        (attention_a, up_a, down_a), (attention_b, up_b, down_b) = [[gather_plain(v) for v in group] for group in shards]
        *heads_a, middle_a = attend(0, attention_a, first, 0)
        hidden_a, pushed_a, second = expand(0, up_a, down_a, middle_a)
        second = exchange(by_patch(second).reshape(blocks))
        *heads_b, middle_b = attend(1, attention_b, second, strip)
        hidden_b, pushed_b, result = expand(1, up_b, down_b, middle_b)
        cot = exchange(by_patch(cotangent[0]).reshape(blocks))
    middle_a, middle_b = middle_a.reshape(tokens, width), middle_b.reshape(tokens, width)
    cot = cot.reshape(tokens, width)

    if fused:
        ffn_cores = lambda: CoreJob(2, width, ffn_weights.shape[-1])
        head_cores = lambda: CoreJob(1, width, kinds * cols)
        grad, *sums_b, kept, result = ffn_backward(
            up_b, down_b, cot, middle_b, pushed_b, hidden_b, mod[1], ffn_cores(),
            [SwapJob(result.reshape(tp, frames, frames, strip, width), True)], 5,
        )
        output = result.reshape(clips.shape)
        ffn_grad = kept
        *more_b, grad, kept, line_up = attention_backward(
            attention_b, grad.reshape(blocks), second, heads_b, mod[1], strip,
            StreamJob(blocks, 0), head_cores(), [ScatterJob([(ffn_grad, 0)], 3 * dp // 8)], 6,
        )
        waiting = [(ffn_grad, 1), (kept, 0)]
        grad, *sums_a, kept, done_up, line_b = ffn_backward(
            up_a, down_a, grad.reshape(pieces), middle_a, pushed_a, hidden_a, mod[0], ffn_cores(),
            [LineJob(line_up), ScatterJob(waiting, dp // 4)], 7,
        )
        ffn_grad = kept
        grad, *more_a, kept, done_b, line_ffn_a, done_up_a = attention_backward(
            attention_a, grad.reshape(first.shape), first, heads_a, mod[0], 0, None, head_cores(),
            [LineJob(line_b), ScatterJob([(ffn_grad, 0), (ffn_grad, 1)], dp // 4, True)], 8,
        )
        packed_a = kept
        done = (done_up_a, done_up, done_b[:1], done_b[1:])
    else:
        result = exchange(result.reshape(blocks)).reshape(pieces)
        output = result.transpose(1, 0, 2, 3).reshape(clips.shape)
        grad, *sums_b, ffn_grad = ffn_backward(up_b, down_b, cot, middle_b, pushed_b, hidden_b, mod[1])
        done_ffn_b = scatter_plain(ffn_grad)
        grad, packed_b, *more_b = attention_backward(
            attention_b, grad.reshape(blocks), second, heads_b, mod[1], strip
        )
        done_b = scatter_plain(packed_b[None])
        grad = exchange(grad.astype(jnp.bfloat16))
        grad, *sums_a, ffn_grad = ffn_backward(up_a, down_a, grad.reshape(pieces), middle_a, pushed_a, hidden_a, mod[0])
        done_ffn_a = scatter_plain(ffn_grad)
        grad, packed_a, *more_a = attention_backward(attention_a, grad.reshape(first.shape), first, heads_a, mod[0], 0)
        done_a = scatter_plain(packed_a[None])
    input_grad = grad.reshape(clips.shape)

    def gather_small(more, sums):
        attention_sums, project_sum = more
        up_sum, low_sums = sums
        return jnp.concatenate(
            [*unpack_bias(project_sum), attention_sums[0], up_sum.reshape(-1), low_sums[0],
             attention_sums[1:].reshape(-1), low_sums[1:].reshape(-1)]
        )

    small = jnp.stack([gather_small(more_a, sums_a), gather_small(more_b, sums_b)])
    token_width = small.shape[1] - mod_width
    *summed, small, grad_act = leave(
        small.reshape(tp, -1, 128), modulation_low, token_width,
        *((packed_a, line_ffn_a, done) if fused else (None, None, None)), 9,
    )
    small = small.transpose(1, 0, 2, 3).reshape(dp, layers, -1)
    grad_mod_low = small[..., token_width:].astype(jnp.bfloat16)
    grad_bias_all = jnp.concatenate(
        [small[..., :token_width], grad_mod_low.astype(jnp.float32)], axis=-1
    ).sum(axis=0)
    grad_bias = lax.dynamic_slice_in_dim(grad_bias_all, position * bias_cols, bias_cols, axis=1)
    grad_mod_weight = dot32("ck,cle->lke", cond_rows, grad_mod_low)[:, :mod_rows]
    grad_act = lax.dynamic_index_in_dim(
        grad_act[:, :, :mod_rows], lax.axis_index("dp"), axis=1, keepdims=False
    )
    if fused:
        grad_attention, grad_ffn = summed
    else:
        grad_attention = jnp.stack([jnp.stack(unpack_heads(done[0])) for done in (done_a, done_b)])
        grad_ffn = jnp.stack([done_ffn_a, done_ffn_b])
    silu_value, silu_pull = jax.vjp(jax.nn.silu, embed)
    cond_grad = silu_pull(grad_act.reshape(1, width))[0]

    return (output, input_grad, cond_grad) + (
        adam_update(attention_weights, attention_first, attention_second, grad_attention, MATRIX_RATE, MATRIX_DECAY)
        + adam_update(ffn_weights, ffn_first, ffn_second, grad_ffn, MATRIX_RATE, MATRIX_DECAY)
        + adam_update(modulation_weights, modulation_first, modulation_second, grad_mod_weight, MATRIX_RATE, MATRIX_DECAY)
        + adam_update(bias_vectors, bias_first, bias_second, grad_bias, VECTOR_RATE, 0.0)
    )


def solution(mesh):
    tokens = P("dp", "tensor", None, None)
    matrix = P(None, None, "dp", "tensor")
    modulation = P(None, BOTH, None)
    vector = P(None, BOTH)
    return jax.shard_map(
        per_device,
        mesh=mesh,
        in_specs=(tokens, tokens, P("dp"), P("dp"), P(), P())
        + (matrix,) * 6 + (modulation,) * 3 + (vector,) * 3,
        out_specs=(tokens, tokens, P("dp", None)) + (matrix,) * 8 + (modulation,) * 4 + (vector,) * 4,
        check_vma=False,
    )
```

profile of v0, /device:TPU:0, one launch (start us, length us, event | category | flops | bytes accessed | tf_op | source)
XLA Modules:
  0.0 505.5 jit_solution(2896452810753593313)
XLA Ops:
  2.0 0.7 convert_element_type.53
  2.7 0.8 fusion.15
  3.5 0.6 fusion.8.row_ref
  4.1 1.3 convert.19
  5.5 0.8 concatenate.39.refs_7_
  6.4 0.8 concatenate.37.refs_0_
  7.2 0.9 pad.14.modulation_ref.refs_7_
  8.1 0.8 slice_bitcast_fusion
  9.0 48.2 %enter.1 = (f32[32,16,128]{2,1,0:T(8,128)}, f32[4,18,128]{2,1,0:T(8,128)}, bf16[4,4,2,96,768]{4,3,2,1,0:T(8,128)(2,1)}, bf16[4,4,2,96,768]{4,3,2,1,0:T(8,128)(2,1)}) custom-call(f32[16,128]{1,0:T(8,128)} %fusion.8.row_ref, bf16[2,32,4608]{2,1,0:T(8,128)(2,1)} %pad.14.modulation_ref.refs_7_, bf16[96,768]{1,0:T(8,128)(2,1)} %concatenate.37.refs_0_, ...), custom_call_target="tpu_custom_call" | custom-call | tf_op jit(solution)/shard_map/enter/pallas_call | solution.py:1372
  57.2 0.8 reshape.268
  58.0 1.0 copy.61
  59.0 1.0 copy.59
  60.7 0.6 squeeze.19.refs_2_.refs_3_.refs_6_
  61.3 0.6 squeeze.17.refs_2_.refs_3_.refs_6_
  61.9 0.6 fusion.26
  62.5 0.6 slice_reduce_fusion.2
  63.4 0.6 broadcast_in_dim.17.refs_3_
  64.3 0.6 copy.44.refs_3_
  64.9 49.0 %attention_forward.2 = (bf16[4,1,4,256,640]{4,3,2,1,0:T(8,128)(2,1)}, bf16[4,1,4,256,256]{4,3,2,1,0:T(8,128)(2,1)}, bf16[1,4,256,768]{3,2,1,0:T(8,128)(2,1)}, f3...) custom-call(bf16[4,768,768]{2,1,0:T(8,128)(2,1)} %bitcast.81, ...), custom_call_target="tpu_custom_call", output_to_operand_aliasing={{4}: (5, {})} | custom-call | flops 7247757312 | bytes 12582912 | tf_op jit(solution)/shard_map/attention_forward/pallas_call | solution.py:1262
  113.9 65.9 %ffn_forward.2 = (bf16[4,1024,768]{2,1,0:T(8,128)(2,1)}, bf16[1024,768]{1,0:T(8,128)(2,1)}, bf16[4,4,64,768]{3,2,1,0:T(8,128)(2,1)}, bf16[4,4,2,96,768]{4,3,2,1,...) custom-call(bf16[4,768,768]{2,1,0:T(8,128)(2,1)} %bitcast.83, ...), custom_call_target="tpu_custom_call", output_to_operand_aliasing={{3}: (6, {})} | custom-call | flops 11596411904 | bytes 11010048 | tf_op jit(solution)/shard_map/ffn_forward/pallas_call | solution.py:1262
  179.9 29.3 %attention_forward.3 = (bf16[4,4,4,64,640]{4,3,2,1,0:T(8,128)(2,1)}, bf16[4,4,4,64,256]{4,3,2,1,0:T(8,128)(2,1)}, bf16[4,4,64,768]{3,2,1,0:T(8,128)(2,1)}, f32[4...) custom-call(bf16[4,768,768]{2,1,0:T(8,128)(2,1)} %bitcast.90, ...), custom_call_target="tpu_custom_call", output_to_operand_aliasing={{4}: (5, {})} | custom-call | flops 7247757312 | bytes 12582912 | tf_op jit(solution)/shard_map/attention_forward/pallas_call | solution.py:1262
  209.2 22.8 %ffn_forward.3 = (bf16[4,1024,768]{2,1,0:T(8,128)(2,1)}, bf16[1024,768]{1,0:T(8,128)(2,1)}, bf16[1024,768]{1,0:T(8,128)(2,1)}, bf16[4,4,4,16,768]{4,3,2,1,0:T(8,128)(2,1)}) custom-call(bf16[4,768,768]{2,1,0:T(8,128)(2,1)} %bitcast.88, bf16[4,768,768]{2,1,0:T(8,128)(2,1)} %bitcast.92, f32[1024,768]{1,0:T(8,128)} %bitcast.98, ...), custom_call_target="tpu_custom_call" | custom-call | flops 11596411904 | bytes 11010048 | tf_op jit(solution)/shard_map/ffn_forward/pallas_call | solution.py:1262
  231.9 38.8 %ffn_backward.2 = (f32[1024,768]{1,0:T(8,128)}, f32[4,1,768]{2,1,0:T(1,128)}, f32[4,768]{1,0:T(4,128)}, bf16[2,2,768,768]{3,2,1,0:T(8,128)(2,1)}, bf16[4,4,4,16,768]{4,3,2,1,0:T(8,128)(2,1)}) custom-call(bf16[4,768,768]{2,1,0:T(8,128)(2,1)} %bitcast.89, bf16[4,768,768]{2,1,0:T(8,128)(2,1)} %bitcast.93, bf16[1024,768]{1,0:T(8,128)(2,1)} %bitcast.102, ...), custom_call_target="tpu_custom_call" | custom-call | flops 23192823808 | bytes 15728640 | tf_op jit(solution)/shard_map/ffn_backward/pallas_call | solution.py:1262
  270.7 52.5 %attention_backward.2 = (f32[4,768]{1,0:T(4,128)}, f32[4,640]{1,0:T(4,128)}, bf16[4,4,64,768]{3,2,1,0:T(8,128)(2,1)}, bf16[1,2,768,768]{3,2,1,0:T(8,128)(2,1)}, bf16[1,4,96,768]{3,2,1,0:T(8,128)(2,1)}) custom-call(bf16[4,768,768]{2,1,0:T(8,128)(2,1)} %bitcast.91, f32[4,4,64,768]{3,2,1,0:T(8,128)} %bitcast.97, ...), custom_call_target="tpu_custom_call" | custom-call | flops 14495514624 | bytes 15728640 | tf_op jit(solution)/shard_map/attention_backward/pallas_call | solution.py:1262
  323.2 47.7 %ffn_backward.3 = (f32[1024,768]{1,0:T(8,128)}, f32[4,1,768]{2,1,0:T(1,128)}, f32[4,768]{1,0:T(4,128)}, bf16[2,2,768,768]{3,2,1,0:T(8,128)(2,1)}, f32[1,96,768]{...) custom-call(bf16[4,768,768]{2,1,0:T(8,128)(2,1)} %bitcast.84, bf16[4,768,768]{2,1,0:T(8,128)(2,1)} %bitcast.87, ...), custom_call_target="tpu_custom_call" | custom-call | flops 23192823808 | bytes 15728640 | tf_op jit(solution)/shard_map/ffn_backward/pallas_call | solution.py:1262
  371.0 57.8 %attention_backward.3 = (f32[1,4,256,768]{3,2,1,0:T(8,128)}, f32[4,768]{1,0:T(4,128)}, f32[4,640]{1,0:T(4,128)}, bf16[1,2,768,768]{3,2,1,0:T(8,128)(2,1)}, f32[2...) custom-call(bf16[4,768,768]{2,1,0:T(8,128)(2,1)} %bitcast.82, ...), custom_call_target="tpu_custom_call" | custom-call | flops 14495514624 | bytes 15728640 | tf_op jit(solution)/shard_map/attention_backward/pallas_call | solution.py:1262
  428.9 0.7 slice_reduce_fusion.9
  429.6 0.7 slice.294
  430.5 0.7 fusion.28
  431.2 0.7 fusion.27
  432.6 0.7 reshape.296.refs_6_
  433.3 1.9 fusion.25
  435.2 51.4 %leave.1 = (f32[2,4,96,192]{3,2,1,0:T(8,128)}, f32[2,2,96,768]{3,2,1,0:T(8,128)}, f32[4,8,42,128]{3,2,1,0:T(8,128)}, f32[32,8,128]{2,1,0:T(8,128)}) custom-call(bf16[1,2,768,768]{3,2,1,0:T(8,128)(2,1)} %get-tuple-element.108.refs_0_, bf16[1,4,96,768]{3,2,1,0:T(8,128)(2,1)} %get-tuple-element.109.refs_1_, f32[1,96,768]{2,1,0:T(8,128)} %get-tuple-element.110.refs_2_, ...), custom_call_target="tpu_custom_call" | custom-call | tf_op jit(solution)/shard_map/leave/pallas_call | solution.py:848
  486.6 1.0 dynamic-slice_reduce_fusion
  487.6 1.4 fusion.10
  489.0 1.2 copy.46
  490.2 0.4 reshape.298
  491.4 0.7 fusion.17
  492.5 2.1 fusion.19
  494.6 0.4 copy-done.11
  495.0 0.4 copy-done.12
  495.4 2.0 fusion.23
  497.4 0.6 copy-done.6
  498.0 0.4 copy-done.7
  498.4 2.6 fusion.21
  501.0 1.1 copy.83
  502.1 1.3 copy-done.2
  503.4 1.7 copy.84
  (128 shorter events, 3.2 us)
Async XLA Ops:
  4.1 3.0 copy-start.1
  6.3 1.8 copy-start
  371.0 59.3 %copy-start.15 = (f32[4,768]{1,0:T(4,128)S(1)}, f32[4,768]{1,0:T(4,128)}, u32[]{:S(2)}) copy-start(f32[4,768]{1,0:T(4,128)} %get-tuple-element.116) | copy-start | bytes 36868
  371.0 59.4 %copy-start.14 = (f32[4,768]{1,0:T(4,128)S(1)}, f32[4,768]{1,0:T(4,128)}, u32[]{:S(2)}) copy-start(f32[4,768]{1,0:T(4,128)} %get-tuple-element.118) | copy-start | bytes 36868
  371.0 59.4 %copy-start.13 = (f32[4,768]{1,0:T(4,128)S(1)}, f32[4,768]{1,0:T(4,128)}, u32[]{:S(2)}) copy-start(f32[4,768]{1,0:T(4,128)} %get-tuple-element.120) | copy-start | bytes 36868
  371.0 61.0 %copy-start.17 = (f32[4,1,768]{2,1,0:T(1,128)S(1)}, f32[4,1,768]{2,1,0:T(1,128)}, u32[]{:S(2)}) copy-start(f32[4,1,768]{2,1,0:T(1,128)} %get-tuple-element.115) | copy-start | bytes 36868
  371.0 61.1 %copy-start.19 = (f32[4,640]{1,0:T(4,128)S(1)}, f32[4,640]{1,0:T(4,128)}, u32[]{:S(2)}) copy-start(f32[4,640]{1,0:T(4,128)} %get-tuple-element.117) | copy-start | bytes 30724
  371.0 61.4 %copy-start.16 = (f32[4,1,768]{2,1,0:T(1,128)S(1)}, f32[4,1,768]{2,1,0:T(1,128)}, u32[]{:S(2)}) copy-start(f32[4,1,768]{2,1,0:T(1,128)} %get-tuple-element.119) | copy-start | bytes 36868
  490.6 0.8 copy-start.18
  490.6 0.8 copy-start.20
  490.6 0.8 copy-start.21
  490.8 1.7 copy-start.8
  490.8 1.7 copy-start.9
  492.5 2.1 copy-start.3
  492.5 2.1 copy-start.10
  492.5 2.5 copy-start.11
  492.5 2.9 copy-start.12
  495.4 2.0 copy-start.5
  495.4 2.6 copy-start.6
  495.4 3.0 copy-start.7
  498.4 2.6 copy-start.4
  501.0 2.5 copy-start.2
where the time goes:
time: 515 us; the launch traced here: 506 us
  Pallas kernels  463 us (90%)
  local copies, waits for them, and re-layouts  26.1 us (5%)
  other arithmetic  12.5 us (2%)
    pallas_call x8, Pallas kernels, call(): pl.pallas_call(kernel, grid=(steps,), in_specs=list(in_specs) + sources,...  364 us
    pallas_call x1, Pallas kernels, leave(): pl.pallas_call(partial(leave_kernel, mod_start), in_specs=([pl.BlockSpec(...  51.4 us
    pallas_call x1, Pallas kernels, enter(): pl.pallas_call(partial(entry_kernel, per_device), in_specs=[inside, insid...  48.2 us

commit v1 on v0

--- a/solution.py
+++ b/solution.py
@@ -381,18 +381,15 @@
     def _():
         def weights(turn, carry):
             rank = turn if cores is None else cores.rank(turn)
-
-            def make():
-                inside = mm(left_ref[0], right_ref[rank])
-                outside = mm(left_ref[1], outer_ref[rank])
-                return jnp.concatenate(
-                    [inside[:, : 4 * PAIR], inside[:, 4 * PAIR :] + outside[:, :PAIR], outside[:, PAIR:]], axis=1
-                )
-
+            inside = mm(left_ref[0], right_ref[rank])
+            outside = mm(left_ref[1], outer_ref[rank])
+            made = jnp.concatenate(
+                [inside[:, : 4 * PAIR], inside[:, 4 * PAIR :] + outside[:, :PAIR], outside[:, PAIR:]], axis=1
+            )
             if cores is None:
-                weight_grad_ref[rank] = make().astype(jnp.bfloat16)
+                weight_grad_ref[rank] = made.astype(jnp.bfloat16)
             else:
-                cores.put(turn, 0, make)
+                cores.put(turn, 0, lambda: made)
                 cores.send(turn, 0)
             return carry
 
@@ -763,7 +760,6 @@
             chains.append(ScatterChain(here, kept.at[0, :, :, part], line, here.count // 2, pick(6)))
             trails.append(LineChain(here, line, out.at[:, part], *pick(2)))
         others = [LineChain(here, begun.at[0], wide_out.at[0, 1], *pick(2))]
-        chains[0].stage_one()
     for step in range(1, tp):
         there = lax.rem(rank + step, tp)
         push(small_ref.at[there], land_ref.at[rank], semaphores.at[0], semaphores.at[1], device, there)
@@ -778,8 +774,6 @@
 
     lax.fori_loop(1, dp, one, 0)
     if scattering:
-        for chain in chains[1:]:
-            chain.stage_one()
         for chain in others:
             chain.start()
     wait_bytes(mine.at[pl.ds(0, dp - 1)], semaphores.at[3])
@@ -787,10 +781,12 @@
         push(mine, mine, semaphores.at[4], semaphores.at[5], device, lax.rem(rank + step, tp))
     if scattering:
         for chain in chains:
-            chain.stage_two()
-        for chain, line in zip(chains, trails):
-            chain.merge()
-            line.start()
+            chain.stage_one()
+        up_first, up_last, down_last, heads_last = done
+        wide_out[0, 0], wide_out[1, 0], wide_out[1, 1] = up_first[0], up_last[0], down_last[0]
+        for kind, value in enumerate(unpack_heads(heads_last[0])):
+            heads_out[1, kind] = value
+        chains[0].stage_two()
     wait_bytes(sum_ref.at[pl.ds(0, tp - 1)], semaphores.at[5])
     layers, padded, columns = modulation_ref.shape
     lines = sum_ref.shape[2]
@@ -810,6 +806,11 @@
 
     lax.fori_loop(1, count, tell, 0)
     if scattering:
+        for chain in chains[1:]:
+            chain.stage_two()
+        for chain, line in zip(chains, trails):
+            chain.merge()
+            line.start()
         for chain in others:
             chain.finish()
     wait_bytes(act_ref.at[pl.ds(0, count - 1)], semaphores.at[7])
@@ -820,12 +821,8 @@
     if scattering:
         for chain in chains + trails:
             chain.finish()
-        up_first, up_last, down_last, heads_last = done
-        wide_out[0, 0], wide_out[1, 0], wide_out[1, 1] = up_first[0], up_last[0], down_last[0]
-        for layer, packed in enumerate((out[...], heads_last[0])):
-            parts = unpack_heads(packed)
-            for kind in range(4):
-                heads_out[layer, kind] = parts[kind]
+        for kind, value in enumerate(unpack_heads(out[...])):
+            heads_out[0, kind] = value
 
 
 def leave(small, modulation, mod_start, kept, begun, done, collective_id):
@@ -1044,8 +1041,8 @@
         two = chains[1]
         if self.close:
             self.stages = {
-                (0, 0): [one.stage_one], (1, 2): [one.stage_two], (2, 0): [one.merge, line.start, two.stage_one],
-                (3, 2): [two.stage_two],
+                (0, 0): [one.stage_one], (1, 1): [one.stage_two], (2, 0): [one.merge, line.start, two.stage_one],
+                (3, 1): [two.stage_two],
             }
             self.last = [line.finish, two.merge, one.finish, two.finish]
             return

time: 515 us -> 512 us (level)
  no operation moved by 1% of the time
where the time goes in v1:
time: 512 us; the launch traced here: 502 us
  Pallas kernels  460 us (90%)
  local copies, waits for them, and re-layouts  26.1 us (5%)
  other arithmetic  12.5 us (2%)
    pallas_call x8, Pallas kernels, call(): pl.pallas_call(kernel, grid=(steps,), in_specs=list(in_specs) + sources,...  359 us
    pallas_call x1, Pallas kernels, leave(): pl.pallas_call(partial(leave_kernel, mod_start), in_specs=([pl.BlockSpec(...  52.2 us
    pallas_call x1, Pallas kernels, enter(): pl.pallas_call(partial(entry_kernel, per_device), in_specs=[inside, insid...  48.2 us

profile of v1, /device:TPU:0, one launch (start us, length us, event | category | flops | bytes accessed | tf_op | source)
XLA Modules:
  0.0 501.9 jit_solution(8337233705043939178)
XLA Ops:
  2.0 0.7 convert_element_type.53
  2.7 0.8 fusion.15
  3.5 0.6 fusion.8.row_ref
  4.1 1.3 convert.19
  5.5 0.8 concatenate.39.refs_7_
  6.4 0.8 concatenate.37.refs_0_
  7.2 0.9 pad.14.modulation_ref.refs_7_
  8.1 0.8 slice_bitcast_fusion
  9.0 48.2 %enter.1 = (f32[32,16,128]{2,1,0:T(8,128)}, f32[4,18,128]{2,1,0:T(8,128)}, bf16[4,4,2,96,768]{4,3,2,1,0:T(8,128)(2,1)}, bf16[4,4,2,96,768]{4,3,2,1,0:T(8,128)(2,1)}) custom-call(f32[16,128]{1,0:T(8,128)} %fusion.8.row_ref, bf16[2,32,4608]{2,1,0:T(8,128)(2,1)} %pad.14.modulation_ref.refs_7_, bf16[96,768]{1,0:T(8,128)(2,1)} %concatenate.37.refs_0_, ...), custom_call_target="tpu_custom_call" | custom-call | tf_op jit(solution)/shard_map/enter/pallas_call | solution.py:1369
  57.2 0.8 reshape.268
  58.0 1.0 copy.61
  59.0 1.0 copy.59
  60.7 0.6 squeeze.19.refs_2_.refs_3_.refs_6_
  61.3 0.6 squeeze.17.refs_2_.refs_3_.refs_6_
  61.9 0.6 fusion.26
  62.5 0.6 slice_reduce_fusion.2
  63.4 0.6 broadcast_in_dim.17.refs_3_
  64.3 0.6 copy.44.refs_3_
  64.9 49.0 %attention_forward.2 = (bf16[4,1,4,256,640]{4,3,2,1,0:T(8,128)(2,1)}, bf16[4,1,4,256,256]{4,3,2,1,0:T(8,128)(2,1)}, bf16[1,4,256,768]{3,2,1,0:T(8,128)(2,1)}, f3...) custom-call(bf16[4,768,768]{2,1,0:T(8,128)(2,1)} %bitcast.81, ...), custom_call_target="tpu_custom_call", output_to_operand_aliasing={{4}: (5, {})} | custom-call | flops 7247757312 | bytes 12582912 | tf_op jit(solution)/shard_map/attention_forward/pallas_call | solution.py:1259
  113.9 65.9 %ffn_forward.2 = (bf16[4,1024,768]{2,1,0:T(8,128)(2,1)}, bf16[1024,768]{1,0:T(8,128)(2,1)}, bf16[4,4,64,768]{3,2,1,0:T(8,128)(2,1)}, bf16[4,4,2,96,768]{4,3,2,1,...) custom-call(bf16[4,768,768]{2,1,0:T(8,128)(2,1)} %bitcast.83, ...), custom_call_target="tpu_custom_call", output_to_operand_aliasing={{3}: (6, {})} | custom-call | flops 11596411904 | bytes 11010048 | tf_op jit(solution)/shard_map/ffn_forward/pallas_call | solution.py:1259
  179.9 29.3 %attention_forward.3 = (bf16[4,4,4,64,640]{4,3,2,1,0:T(8,128)(2,1)}, bf16[4,4,4,64,256]{4,3,2,1,0:T(8,128)(2,1)}, bf16[4,4,64,768]{3,2,1,0:T(8,128)(2,1)}, f32[4...) custom-call(bf16[4,768,768]{2,1,0:T(8,128)(2,1)} %bitcast.90, ...), custom_call_target="tpu_custom_call", output_to_operand_aliasing={{4}: (5, {})} | custom-call | flops 7247757312 | bytes 12582912 | tf_op jit(solution)/shard_map/attention_forward/pallas_call | solution.py:1259
  209.2 22.8 %ffn_forward.3 = (bf16[4,1024,768]{2,1,0:T(8,128)(2,1)}, bf16[1024,768]{1,0:T(8,128)(2,1)}, bf16[1024,768]{1,0:T(8,128)(2,1)}, bf16[4,4,4,16,768]{4,3,2,1,0:T(8,128)(2,1)}) custom-call(bf16[4,768,768]{2,1,0:T(8,128)(2,1)} %bitcast.88, bf16[4,768,768]{2,1,0:T(8,128)(2,1)} %bitcast.92, f32[1024,768]{1,0:T(8,128)} %bitcast.98, ...), custom_call_target="tpu_custom_call" | custom-call | flops 11596411904 | bytes 11010048 | tf_op jit(solution)/shard_map/ffn_forward/pallas_call | solution.py:1259
  232.0 39.0 %ffn_backward.2 = (f32[1024,768]{1,0:T(8,128)}, f32[4,1,768]{2,1,0:T(1,128)}, f32[4,768]{1,0:T(4,128)}, bf16[2,2,768,768]{3,2,1,0:T(8,128)(2,1)}, bf16[4,4,4,16,768]{4,3,2,1,0:T(8,128)(2,1)}) custom-call(bf16[4,768,768]{2,1,0:T(8,128)(2,1)} %bitcast.89, bf16[4,768,768]{2,1,0:T(8,128)(2,1)} %bitcast.93, bf16[1024,768]{1,0:T(8,128)(2,1)} %bitcast.102, ...), custom_call_target="tpu_custom_call" | custom-call | flops 23192823808 | bytes 15728640 | tf_op jit(solution)/shard_map/ffn_backward/pallas_call | solution.py:1259
  271.0 49.3 %attention_backward.2 = (f32[4,768]{1,0:T(4,128)}, f32[4,640]{1,0:T(4,128)}, bf16[4,4,64,768]{3,2,1,0:T(8,128)(2,1)}, bf16[1,2,768,768]{3,2,1,0:T(8,128)(2,1)}, bf16[1,4,96,768]{3,2,1,0:T(8,128)(2,1)}) custom-call(bf16[4,768,768]{2,1,0:T(8,128)(2,1)} %bitcast.91, f32[4,4,64,768]{3,2,1,0:T(8,128)} %bitcast.97, ...), custom_call_target="tpu_custom_call" | custom-call | flops 14495514624 | bytes 15728640 | tf_op jit(solution)/shard_map/attention_backward/pallas_call | solution.py:1259
  320.3 47.8 %ffn_backward.3 = (f32[1024,768]{1,0:T(8,128)}, f32[4,1,768]{2,1,0:T(1,128)}, f32[4,768]{1,0:T(4,128)}, bf16[2,2,768,768]{3,2,1,0:T(8,128)(2,1)}, f32[1,96,768]{...) custom-call(bf16[4,768,768]{2,1,0:T(8,128)(2,1)} %bitcast.84, bf16[4,768,768]{2,1,0:T(8,128)(2,1)} %bitcast.87, ...), custom_call_target="tpu_custom_call" | custom-call | flops 23192823808 | bytes 15728640 | tf_op jit(solution)/shard_map/ffn_backward/pallas_call | solution.py:1259
  368.1 56.2 %attention_backward.3 = (f32[1,4,256,768]{3,2,1,0:T(8,128)}, f32[4,768]{1,0:T(4,128)}, f32[4,640]{1,0:T(4,128)}, bf16[1,2,768,768]{3,2,1,0:T(8,128)(2,1)}, f32[2...) custom-call(bf16[4,768,768]{2,1,0:T(8,128)(2,1)} %bitcast.82, ...), custom_call_target="tpu_custom_call" | custom-call | flops 14495514624 | bytes 15728640 | tf_op jit(solution)/shard_map/attention_backward/pallas_call | solution.py:1259
  424.3 0.7 slice_reduce_fusion.9
  425.0 0.7 slice.294
  425.9 0.7 fusion.28
  426.6 0.7 fusion.27
  428.0 0.7 reshape.296.refs_6_
  428.7 1.9 fusion.25
  430.6 52.2 %leave.1 = (f32[2,4,96,192]{3,2,1,0:T(8,128)}, f32[2,2,96,768]{3,2,1,0:T(8,128)}, f32[4,8,42,128]{3,2,1,0:T(8,128)}, f32[32,8,128]{2,1,0:T(8,128)}) custom-call(bf16[1,2,768,768]{3,2,1,0:T(8,128)(2,1)} %get-tuple-element.108.refs_0_, bf16[1,4,96,768]{3,2,1,0:T(8,128)(2,1)} %get-tuple-element.109.refs_1_, f32[1,96,768]{2,1,0:T(8,128)} %get-tuple-element.110.refs_2_, ...), custom_call_target="tpu_custom_call" | custom-call | tf_op jit(solution)/shard_map/leave/pallas_call | solution.py:845
  482.8 1.0 dynamic-slice_reduce_fusion
  483.9 1.4 fusion.10
  485.3 1.2 copy.46
  486.5 0.4 reshape.298
  487.7 0.7 fusion.17
  488.8 2.1 fusion.19
  490.9 0.4 copy-done.11
  491.3 0.4 copy-done.12
  491.7 2.0 fusion.23
  493.7 0.6 copy-done.6
  494.3 0.4 copy-done.7
  494.7 2.6 fusion.21
  497.3 1.1 copy.83
  498.4 1.3 copy-done.2
  499.7 1.7 copy.84
  (128 shorter events, 3.2 us)
Async XLA Ops:
  4.1 3.0 copy-start.1
  6.3 1.8 copy-start
  368.1 57.7 %copy-start.15 = (f32[4,768]{1,0:T(4,128)S(1)}, f32[4,768]{1,0:T(4,128)}, u32[]{:S(2)}) copy-start(f32[4,768]{1,0:T(4,128)} %get-tuple-element.116) | copy-start | bytes 36868
  368.1 57.7 %copy-start.14 = (f32[4,768]{1,0:T(4,128)S(1)}, f32[4,768]{1,0:T(4,128)}, u32[]{:S(2)}) copy-start(f32[4,768]{1,0:T(4,128)} %get-tuple-element.118) | copy-start | bytes 36868
  368.1 57.8 %copy-start.13 = (f32[4,768]{1,0:T(4,128)S(1)}, f32[4,768]{1,0:T(4,128)}, u32[]{:S(2)}) copy-start(f32[4,768]{1,0:T(4,128)} %get-tuple-element.120) | copy-start | bytes 36868
  368.1 59.4 %copy-start.17 = (f32[4,1,768]{2,1,0:T(1,128)S(1)}, f32[4,1,768]{2,1,0:T(1,128)}, u32[]{:S(2)}) copy-start(f32[4,1,768]{2,1,0:T(1,128)} %get-tuple-element.115) | copy-start | bytes 36868
  368.1 59.5 %copy-start.19 = (f32[4,640]{1,0:T(4,128)S(1)}, f32[4,640]{1,0:T(4,128)}, u32[]{:S(2)}) copy-start(f32[4,640]{1,0:T(4,128)} %get-tuple-element.117) | copy-start | bytes 30724
  368.1 59.7 %copy-start.16 = (f32[4,1,768]{2,1,0:T(1,128)S(1)}, f32[4,1,768]{2,1,0:T(1,128)}, u32[]{:S(2)}) copy-start(f32[4,1,768]{2,1,0:T(1,128)} %get-tuple-element.119) | copy-start | bytes 36868
  486.9 0.8 copy-start.18
  486.9 0.8 copy-start.20
  486.9 0.8 copy-start.21
  487.1 1.7 copy-start.8
  487.1 1.7 copy-start.9
  488.7 2.1 copy-start.3
  488.8 2.1 copy-start.10
  488.8 2.5 copy-start.11
  488.8 2.9 copy-start.12
  491.7 2.0 copy-start.5
  491.7 2.6 copy-start.6
  491.7 3.0 copy-start.7
  494.7 2.6 copy-start.4
  497.3 2.5 copy-start.2

commit v2 on v1

--- a/solution.py
+++ b/solution.py
@@ -1273,9 +1273,9 @@
 
 
 def entry_kernel(
-    per_device, row_ref, modulation_ref, *refs
+    per_device, swap, row_ref, modulation_ref, *refs
 ):
-    gather = 2 if len(refs) > 5 else 0
+    gather = 3 if len(refs) > 5 else 0
     refs = list(refs)
     sources = [refs.pop(0) for _ in range(gather)]
     gathered_ref, mod_ref = refs.pop(0), refs.pop(0)
@@ -1288,6 +1288,7 @@
         here = Where()
         parts = column_parts(here, sources[0], targets[0], space[:PARTS])
         following = GatherChain(here, sources[1], targets[1], space[PARTS])
+        swap.bind(here, sources[2:], targets[2:], space[PARTS + 1 :])
     greet_all()
 
     def tell(index, carry):
@@ -1302,6 +1303,8 @@
     if gather:
         for chain in parts:
             chain.stage_line()
+        for stage in swap.stages[0, 0]:
+            stage()
     wait_bytes(gathered_ref.at[pl.ds(0, count - 1)], semaphores.at[1])
     padded = modulation_ref.shape[1]
     width = dp * tp * per_device
@@ -1358,32 +1361,35 @@
             chain.finish()
         for chain in (*parts, following):
             chain.line_left()
-
-
-def enter(row, modulation, per_device, weights, collective_id):
+        for stage in swap.last:
+            stage()
+
+
+def enter(row, modulation, per_device, weights, swap, collective_id):
     dp, tp = lax.axis_size("dp"), lax.axis_size("tensor")
     count = dp * tp
     lines = modulation.shape[0] * modulation.shape[2] // (tp * PAIR)
     inside = pl.BlockSpec(memory_space=pltpu.VMEM)
     job = FlowJob((), weights) if weights else Job()
+    swap = swap if weights else Job()
     return pl.pallas_call(
-        partial(entry_kernel, per_device),
-        in_specs=[inside, inside] + anywhere(len(job.operands)),
-        out_specs=[inside, inside] + list(job.specs),
+        partial(entry_kernel, per_device, swap),
+        in_specs=[inside, inside] + anywhere(len(job.operands) + len(swap.operands)),
+        out_specs=[inside, inside] + list(job.specs) + list(swap.specs),
         out_shape=[
             jax.ShapeDtypeStruct((count,) + row.shape, jnp.float32),
             jax.ShapeDtypeStruct((tp, lines, PAIR), jnp.float32),
-        ] + list(job.shapes),
+        ] + list(job.shapes) + list(swap.shapes),
         scratch_shapes=[
             pltpu.VMEM((dp, tp, lines, PAIR), jnp.float32),
             pltpu.VMEM((count, lines, PAIR), jnp.float32),
             pltpu.SemaphoreType.DMA((6,)),
-        ] + (GatherChain.scratch() * (PARTS + 1) if weights else []),
+        ] + (GatherChain.scratch() * (PARTS + 1) if weights else []) + list(swap.space),
         compiler_params=pltpu.CompilerParams(
             collective_id=collective_id, has_side_effects=True, vmem_limit_bytes=VMEM_LIMIT
         ),
         name="enter",
-    )(row, modulation, *job.operands)
+    )(row, modulation, *job.operands, *swap.operands)
 
 
 def adam_update(weight, first, second, grad, rate, decay):
@@ -1453,7 +1459,9 @@
     row = jnp.pad(row, (0, -row.shape[0] % 1024)).reshape(-1, 128)
     modulation_low = modulation_weights.astype(jnp.bfloat16)
     modulation_low = jnp.pad(modulation_low, ((0, 0), (0, -mod_rows % 32), (0, 0)))
-    gathered, mod, *begun = enter(row, modulation_low, mod_rows, shards[0][:2] if fused else None, 0)
+    gathered, mod, *begun = enter(row, modulation_low, mod_rows, shards[0][:2] if fused else None,
+        SwapJob(cotangent.reshape(frames, tp, frames, strip, width), False), 0,
+    )
     gathered = gathered.reshape(dp * tp, -1)
     cond_all = gathered[::tp, :width].astype(jnp.bfloat16)
     bias_low = gathered[:, width : width + layers * bias_cols].reshape(dp * tp, layers, bias_cols)
@@ -1482,7 +1490,7 @@
         whole(up), whole(down), middle.reshape(tokens, width), mod[layer], bias_down[layer], bias_up[layer], *more
     )
     if fused:
-        attention_a, up_a = begun
+        attention_a, up_a, cot = begun
         *heads_a, middle_a, up_a, down_a, attention_b = attend(
             0, attention_a, first, 0, [FlowJob([up_a], [shards[1][0]], None, [shards[0][2]])], 1
         )
@@ -1491,10 +1499,7 @@
             [FlowJob([attention_b], [shards[1][2]], dp // 8, [shards[1][1]])], 2, True,
         )
         *heads_b, middle_b, down_b = attend(1, attention_b, second, strip, [FlowJob([down_b], [])], 3)
-        cot = cotangent.reshape(frames, tp, frames, strip, width)
-        hidden_b, pushed_b, result, cot = expand(
-            1, up_b, down_b, middle_b, None, [SwapJob(cot, False)], 4, True
-        )
+        hidden_b, pushed_b, result = expand(1, up_b, down_b, middle_b, None, [], None, True)
         attention_a, up_a, down_a = whole(attention_a), whole(up_a), whole(down_a)
         attention_b, up_b, down_b = whole(attention_b), whole(up_b), whole(down_b)
     else:

time: 512 us -> 512 us (level)
    pallas_call x1, Pallas kernels: 48.2 us -> 54.4 us  [enter(): pl.pallas_call(partial(entry_kernel, per_device, swap), in_specs=[inside,...]
    pallas_call x8, Pallas kernels: 359 us -> 354 us  [call(): pl.pallas_call(kernel, grid=(steps,), in_specs=list(in_specs) + sources,...]
where the time goes in v2:
time: 512 us; the launch traced here: 503 us
  Pallas kernels  461 us (90%)
  local copies, waits for them, and re-layouts  26.1 us (5%)
  other arithmetic  12.5 us (2%)
    pallas_call x8, Pallas kernels, call(): pl.pallas_call(kernel, grid=(steps,), in_specs=list(in_specs) + sources,...  354 us
    pallas_call x1, Pallas kernels, enter(): pl.pallas_call(partial(entry_kernel, per_device, swap), in_specs=[inside,...  54.4 us
    pallas_call x1, Pallas kernels, leave(): pl.pallas_call(partial(leave_kernel, mod_start), in_specs=([pl.BlockSpec(...  52.3 us

profile of v2, /device:TPU:0, one launch (start us, length us, event | category | flops | bytes accessed | tf_op | source)
XLA Modules:
  0.0 502.7 jit_solution(3128536607995974781)
XLA Ops:
  2.0 0.7 convert_element_type.53
  2.7 0.8 fusion.15
  3.5 0.6 fusion.8.row_ref
  4.1 1.3 convert.19
  5.5 0.8 concatenate.39.refs_7_
  6.4 0.8 concatenate.37.refs_0_
  7.2 0.9 pad.14.modulation_ref.refs_7_
  8.1 0.8 slice_bitcast_fusion
  9.0 54.4 %enter.1 = (f32[32,16,128]{2,1,0:T(8,128)}, f32[4,18,128]{2,1,0:T(8,128)}, bf16[4,4,2,96,768]{4,3,2,1,0:T(8,128)(2,1)}, bf16[4,4,2,96,768]{4,3,2,1,0:T(8,128)(2,1)}, bf16[4,4,4,16,768]{4,3,2,1,0:T(8,128)(2,1)}) custom-call(f32[16,128]{1,0:T(8,128)} %fusion.8.row_ref, bf16[2,32,4608]{2,1,0:T(8,128)(2,1)} %pad.14.modulation_ref.refs_7_, ...), custom_call_target="tpu_custom_call" | custom-call | tf_op jit(solution)/shard_map/enter/pallas_call | solution.py:1375
  63.3 0.8 reshape.269
  64.1 1.0 copy.61
  65.2 1.0 copy.59
  66.8 0.6 squeeze.19.refs_2_.refs_3_.refs_6_
  67.4 0.6 squeeze.17.refs_2_.refs_3_.refs_6_
  68.0 0.6 fusion.26
  68.6 0.6 slice_reduce_fusion.2
  69.5 0.6 broadcast_in_dim.17.refs_3_
  70.4 0.6 copy.44.refs_3_
  71.0 47.5 %attention_forward.2 = (bf16[4,1,4,256,640]{4,3,2,1,0:T(8,128)(2,1)}, bf16[4,1,4,256,256]{4,3,2,1,0:T(8,128)(2,1)}, bf16[1,4,256,768]{3,2,1,0:T(8,128)(2,1)}, f3...) custom-call(bf16[4,768,768]{2,1,0:T(8,128)(2,1)} %bitcast.82, ...), custom_call_target="tpu_custom_call", output_to_operand_aliasing={{4}: (5, {})} | custom-call | flops 7247757312 | bytes 12582912 | tf_op jit(solution)/shard_map/attention_forward/pallas_call | solution.py:1259
  118.5 66.5 %ffn_forward.2 = (bf16[4,1024,768]{2,1,0:T(8,128)(2,1)}, bf16[1024,768]{1,0:T(8,128)(2,1)}, bf16[4,4,64,768]{3,2,1,0:T(8,128)(2,1)}, bf16[4,4,2,96,768]{4,3,2,1,...) custom-call(bf16[4,768,768]{2,1,0:T(8,128)(2,1)} %bitcast.84, ...), custom_call_target="tpu_custom_call", output_to_operand_aliasing={{3}: (6, {})} | custom-call | flops 11596411904 | bytes 11010048 | tf_op jit(solution)/shard_map/ffn_forward/pallas_call | solution.py:1259
  184.9 28.9 %attention_forward.3 = (bf16[4,4,4,64,640]{4,3,2,1,0:T(8,128)(2,1)}, bf16[4,4,4,64,256]{4,3,2,1,0:T(8,128)(2,1)}, bf16[4,4,64,768]{3,2,1,0:T(8,128)(2,1)}, f32[4...) custom-call(bf16[4,768,768]{2,1,0:T(8,128)(2,1)} %bitcast.91, ...), custom_call_target="tpu_custom_call", output_to_operand_aliasing={{4}: (5, {})} | custom-call | flops 7247757312 | bytes 12582912 | tf_op jit(solution)/shard_map/attention_forward/pallas_call | solution.py:1259
  213.9 19.2 %ffn_forward.3 = (bf16[4,1024,768]{2,1,0:T(8,128)(2,1)}, bf16[1024,768]{1,0:T(8,128)(2,1)}, bf16[1024,768]{1,0:T(8,128)(2,1)}) custom-call(bf16[4,768,768]{2,1,0:T(8,128)(2,1)} %bitcast.89, bf16[4,768,768]{2,1,0:T(8,128)(2,1)} %bitcast.93, f32[1024,768]{1,0:T(8,128)} %bitcast.99, f32[6,768]{1,0:T(8,128)} %squeeze.19.refs_2_.refs_3_.refs_6_, ...), custom_call_target="tpu_custom_call" | custom-call | flops 11596411904 | bytes 11010048 | tf_op jit(solution)/shard_map/ffn_forward/pallas_call | solution.py:1259
  233.1 39.9 %ffn_backward.2 = (f32[1024,768]{1,0:T(8,128)}, f32[4,1,768]{2,1,0:T(1,128)}, f32[4,768]{1,0:T(4,128)}, bf16[2,2,768,768]{3,2,1,0:T(8,128)(2,1)}, bf16[4,4,4,16,768]{4,3,2,1,0:T(8,128)(2,1)}) custom-call(bf16[4,768,768]{2,1,0:T(8,128)(2,1)} %bitcast.90, bf16[4,768,768]{2,1,0:T(8,128)(2,1)} %bitcast.94, bf16[1024,768]{1,0:T(8,128)(2,1)} %bitcast.86, ...), custom_call_target="tpu_custom_call" | custom-call | flops 23192823808 | bytes 15728640 | tf_op jit(solution)/shard_map/ffn_backward/pallas_call | solution.py:1259
  273.0 48.5 %attention_backward.2 = (f32[4,768]{1,0:T(4,128)}, f32[4,640]{1,0:T(4,128)}, bf16[4,4,64,768]{3,2,1,0:T(8,128)(2,1)}, bf16[1,2,768,768]{3,2,1,0:T(8,128)(2,1)}, bf16[1,4,96,768]{3,2,1,0:T(8,128)(2,1)}) custom-call(bf16[4,768,768]{2,1,0:T(8,128)(2,1)} %bitcast.92, f32[4,4,64,768]{3,2,1,0:T(8,128)} %bitcast.98, ...), custom_call_target="tpu_custom_call" | custom-call | flops 14495514624 | bytes 15728640 | tf_op jit(solution)/shard_map/attention_backward/pallas_call | solution.py:1259
  321.4 47.8 %ffn_backward.3 = (f32[1024,768]{1,0:T(8,128)}, f32[4,1,768]{2,1,0:T(1,128)}, f32[4,768]{1,0:T(4,128)}, bf16[2,2,768,768]{3,2,1,0:T(8,128)(2,1)}, f32[1,96,768]{...) custom-call(bf16[4,768,768]{2,1,0:T(8,128)(2,1)} %bitcast.85, bf16[4,768,768]{2,1,0:T(8,128)(2,1)} %bitcast.88, ...), custom_call_target="tpu_custom_call" | custom-call | flops 23192823808 | bytes 15728640 | tf_op jit(solution)/shard_map/ffn_backward/pallas_call | solution.py:1259
  369.3 55.7 %attention_backward.3 = (f32[1,4,256,768]{3,2,1,0:T(8,128)}, f32[4,768]{1,0:T(4,128)}, f32[4,640]{1,0:T(4,128)}, bf16[1,2,768,768]{3,2,1,0:T(8,128)(2,1)}, f32[2...) custom-call(bf16[4,768,768]{2,1,0:T(8,128)(2,1)} %bitcast.83, ...), custom_call_target="tpu_custom_call" | custom-call | flops 14495514624 | bytes 15728640 | tf_op jit(solution)/shard_map/attention_backward/pallas_call | solution.py:1259
  425.1 0.7 slice_reduce_fusion.9
  425.8 0.7 slice.294
  426.7 0.7 fusion.28
  427.4 0.7 fusion.27
  428.8 0.7 reshape.296.refs_6_
  429.5 1.9 fusion.25
  431.4 52.3 %leave.1 = (f32[2,4,96,192]{3,2,1,0:T(8,128)}, f32[2,2,96,768]{3,2,1,0:T(8,128)}, f32[4,8,42,128]{3,2,1,0:T(8,128)}, f32[32,8,128]{2,1,0:T(8,128)}) custom-call(bf16[1,2,768,768]{3,2,1,0:T(8,128)(2,1)} %get-tuple-element.108.refs_0_, bf16[1,4,96,768]{3,2,1,0:T(8,128)(2,1)} %get-tuple-element.109.refs_1_, f32[1,96,768]{2,1,0:T(8,128)} %get-tuple-element.110.refs_2_, ...), custom_call_target="tpu_custom_call" | custom-call | tf_op jit(solution)/shard_map/leave/pallas_call | solution.py:845
  483.6 1.0 dynamic-slice_reduce_fusion
  484.7 1.4 fusion.10
  486.1 1.2 copy.46
  487.3 0.4 reshape.298
  488.5 0.7 fusion.17
  489.6 2.1 fusion.19
  491.7 0.4 copy-done.11
  492.1 0.4 copy-done.12
  492.5 2.0 fusion.23
  494.5 0.6 copy-done.6
  495.1 0.4 copy-done.7
  495.5 2.6 fusion.21
  498.1 1.1 copy.83
  499.2 1.3 copy-done.2
  500.5 1.7 copy.84
  (128 shorter events, 3.2 us)
Async XLA Ops:
  4.1 3.0 copy-start.1
  6.3 1.8 copy-start
  369.3 57.2 %copy-start.15 = (f32[4,768]{1,0:T(4,128)S(1)}, f32[4,768]{1,0:T(4,128)}, u32[]{:S(2)}) copy-start(f32[4,768]{1,0:T(4,128)} %get-tuple-element.116) | copy-start | bytes 36868
  369.3 57.3 %copy-start.14 = (f32[4,768]{1,0:T(4,128)S(1)}, f32[4,768]{1,0:T(4,128)}, u32[]{:S(2)}) copy-start(f32[4,768]{1,0:T(4,128)} %get-tuple-element.118) | copy-start | bytes 36868
  369.3 57.3 %copy-start.13 = (f32[4,768]{1,0:T(4,128)S(1)}, f32[4,768]{1,0:T(4,128)}, u32[]{:S(2)}) copy-start(f32[4,768]{1,0:T(4,128)} %get-tuple-element.120) | copy-start | bytes 36868
  369.3 58.9 %copy-start.17 = (f32[4,1,768]{2,1,0:T(1,128)S(1)}, f32[4,1,768]{2,1,0:T(1,128)}, u32[]{:S(2)}) copy-start(f32[4,1,768]{2,1,0:T(1,128)} %get-tuple-element.115) | copy-start | bytes 36868
  369.3 59.0 %copy-start.19 = (f32[4,640]{1,0:T(4,128)S(1)}, f32[4,640]{1,0:T(4,128)}, u32[]{:S(2)}) copy-start(f32[4,640]{1,0:T(4,128)} %get-tuple-element.117) | copy-start | bytes 30724
  369.3 59.2 %copy-start.16 = (f32[4,1,768]{2,1,0:T(1,128)S(1)}, f32[4,1,768]{2,1,0:T(1,128)}, u32[]{:S(2)}) copy-start(f32[4,1,768]{2,1,0:T(1,128)} %get-tuple-element.119) | copy-start | bytes 36868
  487.7 0.8 copy-start.18
  487.7 0.8 copy-start.20
  487.7 0.8 copy-start.21
  487.9 1.7 copy-start.8
  487.9 1.7 copy-start.9
  489.6 2.1 copy-start.3
  489.6 2.1 copy-start.10
  489.6 2.5 copy-start.11
  489.6 2.9 copy-start.12
  492.5 2.0 copy-start.5
  492.5 2.6 copy-start.6
  492.5 3.0 copy-start.7
  495.5 2.6 copy-start.4
  498.1 2.5 copy-start.2
